TPU v7x, 256 devices: a whole 4x4x8 slice. The times are simulated.
256 devices in a mesh: frame: 64 (over x, z, core), space: 4 (over y).
Axes of the slice: x: 4, y: 4, z: 8, core: 2. Of those that a mesh axis runs over, the one named last changes fastest.
Arguments:
- queries: bfloat16 [64, 2048, 1152], P('frame', 'space'), may hold values from -2 to 2
- keys: bfloat16 [64, 2048, 1152], P('frame', 'space'), may hold values from -6 to 6
- values: bfloat16 [64, 2048, 1152], P('frame', 'space'), may hold values from -6 to 6
- cotangent: bfloat16 [64, 2048, 1152], P('frame', 'space'), may hold values from -6 to 6
Outputs:
- grad_queries: bfloat16 [64, 2048, 1152], P('frame', 'space')
- grad_keys: bfloat16 [64, 2048, 1152], P('frame', 'space')
- grad_values: bfloat16 [64, 2048, 1152], P('frame', 'space')
All inputs are finite; a program needn't handle non-finite values.
Results may differ from a plain program's by a relative error of at most 0.003.
Values sent between devices are 32-bit elements; how exact they have to be, the bound alone decides.
No kernel may reach another device: no remote copies, remote signals or barrier semaphores. Data moves between devices by JAX's collectives and lax.ppermute only.
A program may use at most 192 MiB of HBM per device.

v0:
```python
import jax
import jax.numpy as jnp
from jax import lax
from jax.sharding import PartitionSpec as P

HEADS = 36
HEAD_DIM = 32


def prefix(value, axis, join, neutral, backward):
    count, mine = (lax.axis_size(axis), lax.axis_index(axis))
    pieces = jax.tree.map(lambda part: lax.all_gather(part, axis), value)
    if backward:
        pieces = jax.tree.map(lambda part: part[::-1], pieces)
        mine = count - 1 - mine
    so_far = jax.tree.map(
        lambda part, zero: jnp.full_like(part, 0) + jnp.asarray(zero, part.dtype), value, neutral
    )

    def step(position, so_far):
        longer = join(so_far, jax.tree.map(lambda part: part[position], pieces))
        return jax.tree.map(lambda new, old: jnp.where(position < mine, new, old), longer, so_far)

    return lax.fori_loop(0, count - 1, step, so_far)


def add_pair(first_terms, second_terms):
    return tuple(
        (first_one + second_one for first_one, second_one in zip(first_terms, second_terms))
    )


def earlier_sum(blocks):
    empty_sums = tuple((jnp.zeros_like(member) for member in blocks))
    return prefix(blocks, "frame", add_pair, empty_sums, False)


def later_sum(blocks):
    empty_sums = tuple((jnp.zeros_like(member) for member in blocks))
    return prefix(blocks, "frame", add_pair, empty_sums, True)


def forward_totals(blocks):
    whole = lax.psum((blocks[0], blocks[1]), "space")
    return add_pair(earlier_sum(whole), whole)


def backward_totals(blocks):
    whole = lax.psum((blocks[0], blocks[1]), "space")
    return add_pair(later_sum(whole), whole)


def shards(queries, keys, values, cotangent):
    highest = lax.Precision.HIGHEST
    tokens = queries.shape[1]
    channels = queries.shape[2]
    frame_tok = tokens * lax.axis_size("space")
    count_now = ((lax.axis_index("frame") + 1) * frame_tok).astype(jnp.float32)
    key_raw = keys[0].reshape(tokens, HEADS, HEAD_DIM)
    key_feat = jnp.maximum(key_raw, 0)
    value_rows = values[0].reshape(tokens, HEADS, HEAD_DIM)
    local_state = jnp.einsum(
        "phi,phj->hij", key_feat, value_rows, preferred_element_type=jnp.float32
    )
    local_norm = jnp.sum(key_feat, axis=0, dtype=jnp.float32)
    state_sum, norm_sum = forward_totals((local_state, local_norm))
    state_now = state_sum / count_now
    norm_now = norm_sum / count_now
    query_raw = queries[0].reshape(tokens, HEADS, HEAD_DIM)
    query_feat = jnp.maximum(query_raw, 0).astype(jnp.float32)
    grad_rows = cotangent[0].reshape(tokens, HEADS, HEAD_DIM).astype(jnp.float32)
    numer = jnp.einsum("phi,hij->phj", query_feat, state_now, precision=highest)
    denom = jnp.einsum("phi,hi->ph", query_feat, norm_now, precision=highest) + 1.0
    output_rows = numer / denom[..., None]
    grad_numer = grad_rows / denom[..., None]
    grad_denom = -jnp.sum(grad_rows * output_rows, axis=-1) / denom
    grad_feat = (
        jnp.einsum("phj,hij->phi", grad_numer, state_now, precision=highest)
        + grad_denom[..., None] * norm_now[None]
    )
    grad_query = (
        jnp.where(query_raw > 0, grad_feat, 0.0).astype(jnp.bfloat16).reshape(1, tokens, channels)
    )
    state_adj = jnp.einsum("phi,phj->hij", query_feat, grad_numer, precision=highest) / count_now
    norm_adj = jnp.einsum("ph,phi->hi", grad_denom, query_feat, precision=highest) / count_now
    later_state, later_norm = backward_totals((state_adj, norm_adj))
    value_wide = value_rows.astype(jnp.float32)
    key_wide = key_feat.astype(jnp.float32)
    grad_key_feat = (
        jnp.einsum("phj,hij->phi", value_wide, later_state, precision=highest) + later_norm[None]
    )
    grad_key = (
        jnp.where(key_raw > 0, grad_key_feat, 0.0).astype(jnp.bfloat16).reshape(1, tokens, channels)
    )
    grad_value = (
        jnp.einsum("phi,hij->phj", key_wide, later_state, precision=highest)
        .astype(jnp.bfloat16)
        .reshape(1, tokens, channels)
    )
    return (grad_query, grad_key, grad_value)


def solution(mesh):
    placed = (
        P("frame", "space", None),
        P("frame", "space", None),
        P("frame", "space", None),
        P("frame", "space", None),
    )
    return jax.shard_map(
        shards,
        mesh=mesh,
        in_specs=placed,
        out_specs=(P("frame", "space", None), P("frame", "space", None), P("frame", "space", None)),
        check_vma=False,
    )
```

profile of v0, /device:TPU:1, one launch (start us, length us, event | category | flops | bytes accessed | tf_op | source)
XLA Modules:
  0.0 866.5 jit_solution(570138433840796354)
XLA Ops:
  7.2 1.6 copy.33
  8.9 2.0 copy.34
  12.2 50.7 %all-reduce.3.cloned.1.call-done = f32[36,32,32]{2,1,0:T(8,128)} async-done(((f32[36,32,32]{2,1,0:T(8,128)}), f32[36,32,32]{2,1,0:T(8,128)}) %all-reduce.3.cloned.1.call-update) | async-done | bytes 147472 | tf_op jit(solution)/shard_map/psum | solution.py:44
  63.4 12.9 %psum.29 = f32[36,32]{1,0:T(8,128)S(1)} all-reduce(f32[36,32]{1,0:T(8,128)S(1)} %reduce_sum.21), channel_id=1, replica_groups=mesh['frame'=64,'space'=4] {'space'}, use_global_device_ids=true, to_apply=%region_2.0 | all-reduce | flops 1152 | bytes 9216 | tf_op jit(solution)/shard_map/psum | solution.py:44
  76.4 2.4 copy.32
  78.8 2.8 copy.37
  81.5 61.8 %all-gather.4 = f32[64,36,32]{1,2,0:T(8,128)} all-gather(f32[1,36,32]{1,2,0:T(8,128)S(1)} %copy.35), channel_id=3, replica_groups=mesh['frame'=64,'space'=4] {'frame'}, dimensions={0}, use_global_device_ids=true | all-gather | bytes 299520 | tf_op jit(solution)/shard_map/all_gather | solution.py:12
  143.4 2.4 broadcast_maximum_fusion
  145.7 76.8 %all-gather.9.cloned.1.call-done = f32[2304,32,32]{2,1,0:T(8,128)} async-done(((f32[36,32,32]{2,1,0:T(8,128)}), f32[2304,32,32]{2,1,0:T(8,128)}) %all-gather.9.cloned.1.call-update) | async-done | bytes 9437200 | tf_op jit(solution)/shard_map/all_gather | solution.py:12
  222.5 133.7 %while.32 = (s32[]{:T(128)}, f32[36,32,32]{2,1,0:T(8,128)S(1)}, f32[36,32]{1,0:T(8,128)S(1)}, s32[]{:T(128)}, f32[64,36,32,32]{3,2,1,0:T(8,128)}, /*index=5*/f32[64,36,32]{1,2,0:T(8,128)}, s32[]{:T(128)}, s32[]{:T(128)}) while((s32[]{:T(128)}, f32[36,32,32]{2,1,0:T(8,128)S(1)}, f32[36,32]{1,0:T(8,128)S(1)}, s32[]{:T(128)}, ...), condition=%wide.region_4.5_spmd.clone, body=%wide.region_3.4_spmd.clone.sunk | while | flops 114052 | bytes 474747 | solution.py:24
  356.2 1.9 fusion.10
  359.4 3.9 convolution_divide_fusion
  363.6 42.7 %all-reduce.5.cloned.1.call-done = f32[36,32,32]{2,1,0:T(8,128)} async-done(((f32[36,32,32]{2,1,0:T(8,128)}), f32[36,32,32]{2,1,0:T(8,128)}) %all-reduce.5.cloned.1.call-update) | async-done | bytes 147472 | tf_op jit(solution)/shard_map/psum | solution.py:49
  409.0 3.3 fusion.4
  412.4 3.5 fusion.3
  415.9 2.4 copy.44
  419.3 13.5 %psum.31 = f32[36,32]{1,0:T(8,128)S(1)} all-reduce(f32[36,32]{1,0:T(8,128)S(1)} %bitcast_divide_fusion.1), channel_id=1, replica_groups=mesh['frame'=64,'space'=4] {'space'}, use_global_device_ids=true, to_apply=%region_7.8 | all-reduce | flops 1152 | bytes 9216 | tf_op jit(solution)/shard_map/psum | solution.py:49
  433.5 56.8 %all-gather.5 = f32[64,36,32]{1,2,0:T(8,128)S(1)} all-gather(f32[1,36,32]{1,2,0:T(8,128)S(1)} %copy.41), channel_id=5, replica_groups=mesh['frame'=64,'space'=4] {'frame'}, dimensions={0}, use_global_device_ids=true | all-gather | bytes 299520 | tf_op jit(solution)/shard_map/all_gather | solution.py:12
  491.4 74.4 %all-gather.11.cloned.1.call-done = f32[2304,32,32]{2,1,0:T(8,128)} async-done(((f32[36,32,32]{2,1,0:T(8,128)}), f32[2304,32,32]{2,1,0:T(8,128)}) %all-gather.11.cloned.1.call-update) | async-done | bytes 9437200 | tf_op jit(solution)/shard_map/all_gather | solution.py:12
  565.8 28.8 %rev.6 = f32[64,36,32,32]{3,2,1,0:T(8,128)} reverse(f32[64,36,32,32]{3,2,1,0:T(8,128)} %bitcast.69), dimensions={0} | reverse | bytes 18874368 | tf_op jit(solution)/shard_map/rev | solution.py:14
  594.6 255.8 %while.33 = (s32[]{:T(128)}, f32[36,32,32]{2,1,0:T(8,128)S(1)}, f32[36,32]{1,0:T(8,128)}, s32[]{:T(128)}, f32[64,36,32,32]{3,2,1,0:T(8,128)}, /*index=5*/f32[64,36,32]{1,2,0:T(8,128)}, s32[]{:T(128)}, s32[]{:T(128)}) while((s32[]{:T(128)}, f32[36,32,32]{2,1,0:T(8,128)S(1)}, f32[36,32]{1,0:T(8,128)}, s32[]{:T(128)}, ...), condition=%wide.region_9.10_spmd.clone, body=%wide.region_8.9_spmd.clone.sunk | while | flops 114052 | bytes 474747 | solution.py:24
  851.8 2.2 convolution_convert_fusion
  853.9 2.4 copy.46
  856.3 2.3 fusion
  (566 shorter events, 397.8 us)
Async XLA Ops:
  7.2 55.7 %all-reduce.3.cloned.1.call-start = ((), (), s32[]{:S(2)}) async-start(), calls=%async_computation | async-start | bytes 1179648 | tf_op jit(solution)/shard_map/psum | solution.py:44
  8.9 2.0 copy-start
  12.2 210.3 %all-gather.9.cloned.1.call-start = ((), (), s32[]{:S(2)}) async-start(), calls=%async_computation.2 | async-start | bytes 38338560 | tf_op jit(solution)/shard_map/all_gather | solution.py:12
  62.9 343.4 %all-reduce.5.cloned.1.call-start = ((), (), s32[]{:S(2)}) async-start(), calls=%async_computation.1 | async-start | bytes 1179648 | tf_op jit(solution)/shard_map/psum | solution.py:49
  356.2 3.3 copy-start.4
  356.2 7.1 copy-start.15
  358.1 0.6 copy-start.7
  358.8 0.6 copy-start.11
  363.3 202.4 %all-gather.11.cloned.1.call-start = ((), (), s32[]{:S(2)}) async-start(), calls=%async_computation.3 | async-start | bytes 38338560 | tf_op jit(solution)/shard_map/all_gather | solution.py:12
  406.3 1.3 copy-start.2
  406.3 1.6 copy-start.12
  407.6 1.3 copy-start.5
  407.6 1.4 copy-start.9
  409.0 3.3 copy-start.8
  409.0 3.3 copy-start.6
  409.0 3.3 copy-start.16
  412.3 3.6 copy-start.13
  415.9 2.4 copy-start.14
  432.8 0.6 copy-start.10
  594.6 257.2 %copy-start.1 = (bf16[1,512,1152]{1,2,0:T(8,128)(2,1)S(1)}, bf16[1,512,1152]{1,2,0:T(8,128)(2,1)}, u32[]{:S(2)}) copy-start(bf16[1,512,1152]{1,2,0:T(8,128)(2,1)} %copy-done) | copy-start | bytes 3538948
  594.6 257.2 %copy-start.3 = (f32[36,32,32]{2,1,0:T(8,128)S(1)}, f32[36,32,32]{2,1,0:T(8,128)}, u32[]{:S(2)}) copy-start(f32[36,32,32]{2,1,0:T(8,128)} %all-reduce.5.cloned.1.call-done) | copy-start | bytes 442372
Sparse Core Ops, SparseCore 0:
  12.3 50.5 all-reduce.2
  65.6 156.7 all-gather.8
  363.5 42.7 all-reduce.4
  408.9 156.8 all-gather.10
where the time goes:
time: 884 us; the launch traced here: 867 us
  other arithmetic  252 us (29%)
  waiting for transfers between devices  245 us (28%)
  local copies, waits for them, and re-layouts  188 us (21%)
  blocking collectives  145 us (16%)
  matrix products  19.4 us (2%)
  between operations  14 us (2%)
    select_n x252, other arithmetic, step(): jnp.where(position < mine, new, old)  246 us
    all_gather x2, waiting for transfers between devices, prefix(): pieces = jax.tree.map(lambda part: lax.all_gather(part, axis), value)  151 us
    dynamic_slice x252, local copies, waits for them, and re-layouts, step(): longer = join(so_far, jax.tree.map(lambda part: part[position], pieces))  140 us
    all_gather x2, blocking collectives, prefix(): pieces = jax.tree.map(lambda part: lax.all_gather(part, axis), value)  119 us
    psum x1, waiting for transfers between devices, forward_totals(): whole = lax.psum((blocks[0], blocks[1]), 'space')  50.7 us
    psum x1, waiting for transfers between devices, backward_totals(): whole = lax.psum((blocks[0], blocks[1]), 'space')  42.7 us
    rev x2, local copies, waits for them, and re-layouts, prefix(): pieces = jax.tree.map(lambda part: part[::-1], pieces)  29.9 us
  transfers between devices with their start and end apart: 4, of which 4 were waited for; matrix products, arithmetic and copies ran while one was open for 2% of the time, Pallas kernels for 0%

commit v1 on v0

v1 whole, which is shorter than its diff:
```python
import jax
import jax.numpy as jnp
from jax import lax
from jax.experimental import pallas as pl
from jax.experimental.pallas import tpu as pltpu
from jax.sharding import PartitionSpec as P

HEAD_DIM = 32
LANES = 128
GROUPS = 9
STEPS = 3
PER_STEP = GROUPS // STEPS
STATE_ROWS = GROUPS * HEAD_DIM
ROWS = 512
FRAME_TOK = 2048

ROW_BY_ROW = (((0,), (0,)), ((), ()))
LANE_BY_LANE = (((1,), (1,)), ((), ()))
PLAIN = (((1,), (0,)), ((), ()))


def dot(lhs, rhs, dims):
    return lax.dot_general(lhs, rhs, dims, preferred_element_type=jnp.float32)


def halves(wide):
    high = wide.astype(jnp.bfloat16)
    low = (wide - high.astype(jnp.float32)).astype(jnp.bfloat16)
    return high, low


def same_head():
    row = lax.broadcasted_iota(jnp.int32, (LANES, LANES), 0)
    lane = lax.broadcasted_iota(jnp.int32, (LANES, LANES), 1)
    return (row // HEAD_DIM) == (lane // HEAD_DIM)


def spread(compact, same):
    return jnp.where(same, jnp.concatenate([compact] * (LANES // HEAD_DIM), axis=0), 0.0)


def gather_heads(full, same):
    full = jnp.where(same, full, 0.0)
    parts = [full[h * HEAD_DIM : (h + 1) * HEAD_DIM] for h in range(LANES // HEAD_DIM)]
    return (parts[0] + parts[1]) + (parts[2] + parts[3])


def block_kernel(key_ref, value_ref, out_ref):
    step = pl.program_id(0)
    same = same_head()

    @pl.when(step == 0)
    def _():
        out_ref[STATE_ROWS:, :] = jnp.zeros((ROWS - STATE_ROWS, LANES), jnp.float32)

    for part in range(PER_STEP):
        group = step * PER_STEP + part
        lanes = slice(part * LANES, (part + 1) * LANES)
        feat = jnp.maximum(key_ref[0, :, lanes], 0)
        full = dot(feat, value_ref[0, :, lanes], ROW_BY_ROW)
        out_ref[pl.ds(group * HEAD_DIM, HEAD_DIM), :] = gather_heads(full, same)
        out_ref[pl.ds(STATE_ROWS + group, 1), :] = jnp.sum(
            feat.astype(jnp.float32), axis=0, keepdims=True
        )


def scan_kernel(backward, sent_ref, out_ref):
    devices = ROWS // 2
    row = lax.broadcasted_iota(jnp.int32, (devices, devices), 0) // 4
    col = lax.broadcasted_iota(jnp.int32, (devices, devices), 1) // 4
    pick = (col >= row) if backward else (col <= row)
    pick = jnp.where(pick, 1.0, 0.0).astype(jnp.bfloat16)
    frame = lax.broadcasted_iota(jnp.int32, (devices, LANES), 0) // 4
    count = ((frame + 1) * FRAME_TOK).astype(jnp.float32)
    for half in range(2):
        rows = pl.ds(half, devices, stride=2)
        terms = sent_ref[rows, :]
        if backward:
            terms = terms / count
        high = terms.astype(jnp.bfloat16)
        rest = terms - high.astype(jnp.float32)
        middle, low = halves(rest)
        total = dot(pick, low, PLAIN) + dot(pick, middle, PLAIN) + dot(pick, high, PLAIN)
        if not backward:
            total = total / count
        out_ref[rows, :] = total


def query_kernel(query_ref, grad_ref, state_ref, out_ref, adj_ref):
    step = pl.program_id(0)
    same = same_head()
    ones = jnp.where(same, 1.0, 0.0).astype(jnp.bfloat16)

    @pl.when(step == 0)
    def _():
        adj_ref[STATE_ROWS:, :] = jnp.zeros((ROWS - STATE_ROWS, LANES), jnp.float32)

    for part in range(PER_STEP):
        group = step * PER_STEP + part
        lanes = slice(part * LANES, (part + 1) * LANES)
        state = spread(state_ref[pl.ds(group * HEAD_DIM, HEAD_DIM), :], same)
        norm = state_ref[pl.ds(STATE_ROWS + group, 1), :]
        state_high, state_low = halves(state)
        norm_high, norm_low = halves(jnp.where(same, norm, 0.0))
        query = query_ref[0, :, lanes]
        grad = grad_ref[0, :, lanes]
        feat = jnp.maximum(query, 0)
        denom = dot(feat, norm_low, LANE_BY_LANE) + dot(feat, norm_high, LANE_BY_LANE) + 1.0
        back = dot(grad, state_low, LANE_BY_LANE) + dot(grad, state_high, LANE_BY_LANE)
        feat_wide = feat.astype(jnp.float32)
        scale = 1.0 / denom
        high, low = halves(feat_wide * back)
        along = dot(low, ones, PLAIN) + dot(high, ones, PLAIN)
        grad_denom = -(along * scale) * scale
        grad_feat = back * scale + grad_denom * norm
        out_ref[0, :, lanes] = jnp.where(
            query.astype(jnp.float32) > 0, grad_feat, 0.0
        ).astype(jnp.bfloat16)
        high, low = halves(grad.astype(jnp.float32) * scale)
        full = dot(feat, low, ROW_BY_ROW) + dot(feat, high, ROW_BY_ROW)
        adj_ref[pl.ds(group * HEAD_DIM, HEAD_DIM), :] = gather_heads(full, same)
        adj_ref[pl.ds(STATE_ROWS + group, 1), :] = jnp.sum(
            grad_denom * feat_wide, axis=0, keepdims=True
        )


def key_kernel(key_ref, value_ref, state_ref, grad_key_ref, grad_value_ref):
    step = pl.program_id(0)
    same = same_head()
    for part in range(PER_STEP):
        group = step * PER_STEP + part
        lanes = slice(part * LANES, (part + 1) * LANES)
        state = spread(state_ref[pl.ds(group * HEAD_DIM, HEAD_DIM), :], same)
        norm = state_ref[pl.ds(STATE_ROWS + group, 1), :]
        high, low = halves(state)
        key = key_ref[0, :, lanes]
        value = value_ref[0, :, lanes]
        feat = jnp.maximum(key, 0)
        grad_feat = dot(value, low, LANE_BY_LANE) + dot(value, high, LANE_BY_LANE) + norm
        grad_key_ref[0, :, lanes] = jnp.where(
            key.astype(jnp.float32) > 0, grad_feat, 0.0
        ).astype(jnp.bfloat16)
        grad_value = dot(feat, low, PLAIN) + dot(feat, high, PLAIN)
        grad_value_ref[0, :, lanes] = grad_value.astype(jnp.bfloat16)


def shards(queries, keys, values, cotangent):
    tokens, channels = queries.shape[1:]
    rows_spec = pl.BlockSpec((1, tokens, PER_STEP * LANES), lambda step: (0, 0, step))
    whole_spec = pl.BlockSpec((ROWS, LANES), lambda step: (0, 0))
    rows_shape = jax.ShapeDtypeStruct((1, tokens, channels), jnp.bfloat16)
    whole_shape = jax.ShapeDtypeStruct((ROWS, LANES), jnp.float32)
    params = pltpu.CompilerParams(vmem_limit_bytes=32 * 1024 * 1024)

    def exchange(whole):
        pieces = whole.reshape(ROWS // 2, 2, LANES)
        pieces = lax.all_to_all(pieces, ("frame", "space"), 0, 0, tiled=True)
        return pieces.reshape(ROWS, LANES)

    def scan(whole, backward):
        return pl.pallas_call(
            lambda sent_ref, out_ref: scan_kernel(backward, sent_ref, out_ref),
            out_shape=whole_shape,
            compiler_params=params,
            name="later" if backward else "earlier",
        )(whole)

    blocks = pl.pallas_call(
        block_kernel,
        grid=(STEPS,),
        in_specs=[rows_spec, rows_spec],
        out_specs=whole_spec,
        out_shape=whole_shape,
        compiler_params=params,
        name="blocks",
    )(keys, values)
    state = exchange(scan(exchange(blocks), False))
    grad_query, adjoint = pl.pallas_call(
        query_kernel,
        grid=(STEPS,),
        in_specs=[rows_spec, rows_spec, whole_spec],
        out_specs=(rows_spec, whole_spec),
        out_shape=(rows_shape, whole_shape),
        compiler_params=params,
        name="queries",
    )(queries, cotangent, state)
    later = exchange(scan(exchange(adjoint), True))
    grad_key, grad_value = pl.pallas_call(
        key_kernel,
        grid=(STEPS,),
        in_specs=[rows_spec, rows_spec, whole_spec],
        out_specs=(rows_spec, rows_spec),
        out_shape=(rows_shape, rows_shape),
        compiler_params=params,
        name="keys",
    )(keys, values, later)
    return (grad_query, grad_key, grad_value)


def solution(mesh):
    placed = P("frame", "space", None)
    return jax.shard_map(
        shards,
        mesh=mesh,
        in_specs=(placed,) * 4,
        out_specs=(placed,) * 3,
        check_vma=False,
    )
```

time: 884 us -> 109 us (0.12); the launches traced: 867 us -> 109 us
  other arithmetic: 252 us -> 0 us
  waiting for transfers between devices: 245 us -> 0 us
  local copies, waits for them, and re-layouts: 188 us -> 2.55 us
  blocking collectives: 145 us -> 94.9 us
  matrix products: 19.4 us -> 0 us
  between operations: 14 us -> 0.67 us
  Pallas kernels: 0 us -> 10.4 us
    select_n x252 -> x0, other arithmetic: 246 us -> none  [step(): jnp.where(position < mine, new, old)]
    all_gather x2 -> x0, waiting for transfers between devices: 151 us -> none  [prefix(): pieces = jax.tree.map(lambda part: lax.all_gather(part, axis), value)]
    dynamic_slice x252 -> x0, local copies, waits for them, and re-layouts: 140 us -> none  [step(): longer = join(so_far, jax.tree.map(lambda part: part[position], pieces))]
    all_gather x2 -> x0, blocking collectives: 119 us -> none  [prefix(): pieces = jax.tree.map(lambda part: lax.all_gather(part, axis), value)]
    all_to_all x0 -> x4, blocking collectives: none -> 94.9 us  [exchange(): pieces = lax.all_to_all(pieces, ('frame', 'space'), 0, 0, tiled=True)]
    psum x2 -> x0, waiting for transfers between devices: 93.4 us -> none  [the longest x1 50.7 us: forward_totals(): whole = lax.psum((blocks[0], blocks[1]), 'space')]
    rev x2 -> x0, local copies, waits for them, and re-layouts: 29.9 us -> none  [prefix(): pieces = jax.tree.map(lambda part: part[::-1], pieces)]
    psum x2 -> x0, blocking collectives: 26.4 us -> none  [the longest x1 13.5 us: backward_totals(): whole = lax.psum((blocks[0], blocks[1]), 'space')]
  transfers between devices with their start and end apart: 4 -> 0, of which waited for: 4 -> 0; matrix products, arithmetic and copies ran while one was open for 2% -> 0% of each run, Pallas kernels for 0% -> 0%
where the time goes in v1:
time: 109 us
  blocking collectives  94.9 us (87%)
  Pallas kernels  10.4 us (10%)
  local copies, waits for them, and re-layouts  2.55 us (2%)
    all_to_all x4, blocking collectives, exchange(): pieces = lax.all_to_all(pieces, ('frame', 'space'), 0, 0, tiled=True)  94.9 us
    pallas_call x1, Pallas kernels, shards(): pl.pallas_call(query_kernel, grid=(STEPS,), in_specs=[rows_spec, rows_spe...  5.21 us
    pallas_call x1, Pallas kernels, shards(): pl.pallas_call(key_kernel, grid=(STEPS,), in_specs=[rows_spec, rows_spec,...  3.07 us
    unnamed x12, local copies, waits for them, and re-layouts  2.55 us

profile of v1, /device:TPU:1, one launch (start us, length us, event | category | flops | bytes accessed | tf_op | source)
XLA Modules:
  0.0 108.6 jit_solution(15933564463663924934)
XLA Ops:
  0.6 0.0 copy-start
  0.6 1.3 %copy-done = bf16[1,512,1152]{2,1,0:T(8,128)(2,1)S(1)} copy-done((bf16[1,512,1152]{2,1,0:T(8,128)(2,1)S(1)}, bf16[1,512,1152]{2,1,0:T(8,128)(2,1)}, u32[]{:S(2)}) %copy-start) | copy-done | bytes 1179672
  1.9 0.0 copy-start.2
  1.9 1.3 %copy-done.2 = bf16[1,512,1152]{2,1,0:T(8,128)(2,1)S(1)} copy-done((bf16[1,512,1152]{2,1,0:T(8,128)(2,1)S(1)}, bf16[1,512,1152]{2,1,0:T(8,128)(2,1)}, u32[]{:S(2)}) %copy-start.2) | copy-done | bytes 1179672
  3.2 0.0 copy-start.5
  3.2 1.3 %blocks.1 = f32[512,128]{1,0:T(8,128)S(1)} custom-call(bf16[1,512,1152]{2,1,0:T(8,128)(2,1)S(1)} %copy-done, bf16[1,512,1152]{2,1,0:T(8,128)(2,1)S(1)} %copy-done.2), custom_call_target="tpu_custom_call" | custom-call | tf_op jit(solution)/shard_map/blocks/pallas_call | solution.py:168
  4.5 0.0 copy-start.4
  4.5 31.2 %all_to_all.20 = f32[256,2,128]{2,1,0:T(2,128)S(1)} all-to-all(f32[256,2,128]{2,1,0:T(2,128)S(1)} %bitcast.10), channel_id=1, replica_groups=mesh['frame'=64,'space'=4] {'frame','space'}, dimensions={0} | all-to-all | bytes 524288 | tf_op jit(solution)/shard_map/all_to_all | solution.py:157
  35.7 0.4 earlier.1
  36.1 21.2 %all_to_all.21 = f32[256,2,128]{2,1,0:T(2,128)S(1)} all-to-all(f32[256,2,128]{2,1,0:T(2,128)S(1)} %bitcast.12), channel_id=1, replica_groups=mesh['frame'=64,'space'=4] {'frame','space'}, dimensions={0} | all-to-all | bytes 524288 | tf_op jit(solution)/shard_map/all_to_all | solution.py:157
  57.3 0.0 copy-done.5
  57.3 0.0 copy-done.4
  57.3 0.0 copy-start.3
  57.3 5.2 %queries.1 = (bf16[1,512,1152]{2,1,0:T(8,128)(2,1)}, f32[512,128]{1,0:T(8,128)S(1)}) custom-call(bf16[1,512,1152]{2,1,0:T(8,128)(2,1)S(1)} %copy-done.4, bf16[1,512,1152]{2,1,0:T(8,128)(2,1)S(1)} %copy-done.5, f32[512,128]{1,0:T(8,128)S(1)} %bitcast.8), custom_call_target="tpu_custom_call" | custom-call | tf_op jit(solution)/shard_map/queries/pallas_call | solution.py:178
  62.5 0.0 copy-start.1
  62.5 21.3 %all_to_all.22 = f32[256,2,128]{2,1,0:T(2,128)S(1)} all-to-all(f32[256,2,128]{2,1,0:T(2,128)S(1)} %bitcast.15), channel_id=1, replica_groups=mesh['frame'=64,'space'=4] {'frame','space'}, dimensions={0} | all-to-all | bytes 524288 | tf_op jit(solution)/shard_map/all_to_all | solution.py:157
  83.9 0.4 later.1
  84.3 21.2 %all_to_all.23 = f32[256,2,128]{2,1,0:T(2,128)S(1)} all-to-all(f32[256,2,128]{2,1,0:T(2,128)S(1)} %bitcast.14), channel_id=1, replica_groups=mesh['frame'=64,'space'=4] {'frame','space'}, dimensions={0} | all-to-all | bytes 524288 | tf_op jit(solution)/shard_map/all_to_all | solution.py:157
  105.5 0.0 copy-done.3
  105.5 0.0 copy-done.1
  105.5 3.1 %keys.1 = (bf16[1,512,1152]{2,1,0:T(8,128)(2,1)}, bf16[1,512,1152]{2,1,0:T(8,128)(2,1)}) custom-call(bf16[1,512,1152]{2,1,0:T(8,128)(2,1)S(1)} %copy-done.1, bf16[1,512,1152]{2,1,0:T(8,128)(2,1)S(1)} %copy-done.3, f32[512,128]{1,0:T(8,128)S(1)} %bitcast.9), custom_call_target="tpu_custom_call" | custom-call | tf_op jit(solution)/shard_map/keys/pallas_call | solution.py:188
Async XLA Ops:
  0.6 1.3 %copy-start = (bf16[1,512,1152]{2,1,0:T(8,128)(2,1)S(1)}, bf16[1,512,1152]{2,1,0:T(8,128)(2,1)}, u32[]{:S(2)}) copy-start(bf16[1,512,1152]{2,1,0:T(8,128)(2,1)} %key_ref.3) | copy-start | bytes 3538948
  1.9 1.3 %copy-start.2 = (bf16[1,512,1152]{2,1,0:T(8,128)(2,1)S(1)}, bf16[1,512,1152]{2,1,0:T(8,128)(2,1)}, u32[]{:S(2)}) copy-start(bf16[1,512,1152]{2,1,0:T(8,128)(2,1)} %value_ref.3) | copy-start | bytes 3538948
  3.2 54.1 %copy-start.5 = (bf16[1,512,1152]{2,1,0:T(8,128)(2,1)S(1)}, bf16[1,512,1152]{2,1,0:T(8,128)(2,1)}, u32[]{:S(2)}) copy-start(bf16[1,512,1152]{2,1,0:T(8,128)(2,1)} %grad_ref.1) | copy-start | bytes 3538948
  4.5 52.8 %copy-start.4 = (bf16[1,512,1152]{2,1,0:T(8,128)(2,1)S(1)}, bf16[1,512,1152]{2,1,0:T(8,128)(2,1)}, u32[]{:S(2)}) copy-start(bf16[1,512,1152]{2,1,0:T(8,128)(2,1)} %query_ref.1) | copy-start | bytes 3538948
  57.3 48.2 %copy-start.3 = (bf16[1,512,1152]{2,1,0:T(8,128)(2,1)S(1)}, bf16[1,512,1152]{2,1,0:T(8,128)(2,1)}, u32[]{:S(2)}) copy-start(bf16[1,512,1152]{2,1,0:T(8,128)(2,1)} %value_ref.3) | copy-start | bytes 3538948
  62.5 43.0 %copy-start.1 = (bf16[1,512,1152]{2,1,0:T(8,128)(2,1)S(1)}, bf16[1,512,1152]{2,1,0:T(8,128)(2,1)}, u32[]{:S(2)}) copy-start(bf16[1,512,1152]{2,1,0:T(8,128)(2,1)} %key_ref.3) | copy-start | bytes 3538948

commit v2 on v1

--- a/solution.py
+++ b/solution.py
@@ -3,6 +3,7 @@
 from jax import lax
 from jax.experimental import pallas as pl
 from jax.experimental.pallas import tpu as pltpu
+from jax.sharding import Mesh
 from jax.sharding import PartitionSpec as P
 
 HEAD_DIM = 32
@@ -11,7 +12,9 @@
 STEPS = 3
 PER_STEP = GROUPS // STEPS
 STATE_ROWS = GROUPS * HEAD_DIM
-ROWS = 512
+X, Z, CORES, SPACE = 4, 8, 2, 4
+CHUNK = 40
+ROWS = CORES * SPACE * CHUNK
 FRAME_TOK = 2048
 
 ROW_BY_ROW = (((0,), (0,)), ((), ()))
@@ -64,32 +67,76 @@
         )
 
 
-def scan_kernel(backward, sent_ref, out_ref):
-    devices = ROWS // 2
-    row = lax.broadcasted_iota(jnp.int32, (devices, devices), 0) // 4
-    col = lax.broadcasted_iota(jnp.int32, (devices, devices), 1) // 4
-    pick = (col >= row) if backward else (col <= row)
-    pick = jnp.where(pick, 1.0, 0.0).astype(jnp.bfloat16)
-    frame = lax.broadcasted_iota(jnp.int32, (devices, LANES), 0) // 4
-    count = ((frame + 1) * FRAME_TOK).astype(jnp.float32)
-    for half in range(2):
-        rows = pl.ds(half, devices, stride=2)
-        terms = sent_ref[rows, :]
-        if backward:
-            terms = terms / count
-        high = terms.astype(jnp.bfloat16)
-        rest = terms - high.astype(jnp.float32)
-        middle, low = halves(rest)
-        total = dot(pick, low, PLAIN) + dot(pick, middle, PLAIN) + dot(pick, high, PLAIN)
+def wrapped(position, shift, size):
+    return (position + shift + size) % size
+
+
+def counted(keep, term):
+    return jnp.where(keep, term, 0.0)
+
+
+def precedes(backward, other, mine):
+    return (other > mine) if backward else (other < mine)
+
+
+def chip_kernel(backward, pieces_ref, edge_ref, both_ref):
+    def core(number):
+        base = number * SPACE * CHUNK
+        parts = [pieces_ref[base + s * CHUNK : base + (s + 1) * CHUNK, :] for s in range(SPACE)]
+        return (parts[0] + parts[1]) + (parts[2] + parts[3])
+
+    first, second = core(0), core(1)
+    edge_ref[...] = second if backward else first
+    both_ref[...] = first + second
+
+
+def window_kernel(backward, mine_ref, below_ref, above_ref, up_ref, down_ref):
+    z = lax.axis_index("z")
+    window = ((-1, below_ref[...]), (0, mine_ref[...]), (1, above_ref[...]))
+    for out_ref, shift, members in ((up_ref, 3, window), (down_ref, -3, window[:2])):
+        target = wrapped(z, shift, Z)
+        masked = whole = None
+        for offset, term in members:
+            kept = counted(precedes(backward, wrapped(z, offset, Z), target), term)
+            masked = kept if masked is None else masked + kept
+            whole = term if whole is None else whole + term
+        out_ref[:CHUNK, :] = masked
+        out_ref[CHUNK:, :] = whole
+
+
+def line_kernel(backward, mine_ref, below_ref, above_ref, lower_ref, upper_ref, masked_ref, whole_ref):
+    z = lax.axis_index("z")
+    below, above = below_ref[...], above_ref[...]
+    near = counted(precedes(backward, wrapped(z, -1, Z), z), below) + counted(
+        precedes(backward, wrapped(z, 1, Z), z), above
+    )
+    masked_ref[...] = near + (lower_ref[:CHUNK, :] + upper_ref[:CHUNK, :])
+    whole_ref[...] = (below + mine_ref[...] + above) + (lower_ref[CHUNK:, :] + upper_ref[CHUNK:, :])
+
+
+def frame_kernel(backward, line_ref, edge_ref, both_ref, *refs):
+    x, z = lax.axis_index("x"), lax.axis_index("z")
+    out_ref = refs[-1]
+    total = line_ref[...]
+    for shift, ref in enumerate(refs[:-1], 1):
+        total = total + counted(precedes(backward, wrapped(x, -shift, X), x), ref[...])
+    edge, both = total + edge_ref[...], total + both_ref[...]
+    frames = (both, edge) if backward else (edge, both)
+    for core, frame in enumerate(frames):
         if not backward:
-            total = total / count
-        out_ref[rows, :] = total
+            count = ((x * Z + z) * 2 + core + 1) * FRAME_TOK
+            frame = frame / count.astype(jnp.float32)
+        for s in range(SPACE):
+            base = (core * SPACE + s) * CHUNK
+            out_ref[base : base + CHUNK, :] = frame
 
 
 def query_kernel(query_ref, grad_ref, state_ref, out_ref, adj_ref):
     step = pl.program_id(0)
     same = same_head()
     ones = jnp.where(same, 1.0, 0.0).astype(jnp.bfloat16)
+    frame = (lax.axis_index("x") * Z + lax.axis_index("z")) * CORES + lax.axis_index("c")
+    count = ((frame + 1) * FRAME_TOK).astype(jnp.float32)
 
     @pl.when(step == 0)
     def _():
@@ -118,9 +165,9 @@
         ).astype(jnp.bfloat16)
         high, low = halves(grad.astype(jnp.float32) * scale)
         full = dot(feat, low, ROW_BY_ROW) + dot(feat, high, ROW_BY_ROW)
-        adj_ref[pl.ds(group * HEAD_DIM, HEAD_DIM), :] = gather_heads(full, same)
-        adj_ref[pl.ds(STATE_ROWS + group, 1), :] = jnp.sum(
-            grad_denom * feat_wide, axis=0, keepdims=True
+        adj_ref[pl.ds(group * HEAD_DIM, HEAD_DIM), :] = gather_heads(full, same) / count
+        adj_ref[pl.ds(STATE_ROWS + group, 1), :] = (
+            jnp.sum(grad_denom * feat_wide, axis=0, keepdims=True) / count
         )
 
 
@@ -152,18 +199,36 @@
     whole_shape = jax.ShapeDtypeStruct((ROWS, LANES), jnp.float32)
     params = pltpu.CompilerParams(vmem_limit_bytes=32 * 1024 * 1024)
 
+    def small(kernel, backward, name, shapes, *args):
+        shapes = tuple(jax.ShapeDtypeStruct((rows, LANES), jnp.float32) for rows in shapes)
+        return pl.pallas_call(
+            lambda *refs: kernel(backward, *refs),
+            out_shape=shapes,
+            compiler_params=params,
+            name=name + ("_later" if backward else "_earlier"),
+        )(*args)
+
     def exchange(whole):
-        pieces = whole.reshape(ROWS // 2, 2, LANES)
-        pieces = lax.all_to_all(pieces, ("frame", "space"), 0, 0, tiled=True)
+        pieces = whole.reshape(CORES * SPACE, CHUNK, LANES)
+        pieces = lax.all_to_all(pieces, ("c", "space"), 0, 0, tiled=True)
         return pieces.reshape(ROWS, LANES)
 
+    def shift(value, axis, size, by):
+        return lax.ppermute(value, axis, [(i, (i + by) % size) for i in range(size)])
+
     def scan(whole, backward):
-        return pl.pallas_call(
-            lambda sent_ref, out_ref: scan_kernel(backward, sent_ref, out_ref),
-            out_shape=whole_shape,
-            compiler_params=params,
-            name="later" if backward else "earlier",
-        )(whole)
+        edge, both = small(chip_kernel, backward, "chip", (CHUNK, CHUNK), exchange(whole))
+        below, above = (shift(both, "z", Z, by) for by in (1, -1))
+        up, down = small(
+            window_kernel, backward, "window", (2 * CHUNK, 2 * CHUNK), both, below, above
+        )
+        lower, upper = shift(up, "z", Z, 3), shift(down, "z", Z, -3)
+        masked, total = small(
+            line_kernel, backward, "line", (CHUNK, CHUNK), both, below, above, lower, upper
+        )
+        others = [shift(total, "x", X, by) for by in (1, 2, 3)]
+        (frames,) = small(frame_kernel, backward, "frame", (ROWS,), masked, edge, both, *others)
+        return exchange(frames)
 
     blocks = pl.pallas_call(
         block_kernel,
@@ -174,7 +239,7 @@
         compiler_params=params,
         name="blocks",
     )(keys, values)
-    state = exchange(scan(exchange(blocks), False))
+    state = scan(blocks, False)
     grad_query, adjoint = pl.pallas_call(
         query_kernel,
         grid=(STEPS,),
@@ -184,7 +249,7 @@
         compiler_params=params,
         name="queries",
     )(queries, cotangent, state)
-    later = exchange(scan(exchange(adjoint), True))
+    later = scan(adjoint, True)
     grad_key, grad_value = pl.pallas_call(
         key_kernel,
         grid=(STEPS,),
@@ -198,10 +263,11 @@
 
 
 def solution(mesh):
-    placed = P("frame", "space", None)
+    split = Mesh(mesh.devices.reshape(X, Z, CORES, SPACE), ("x", "z", "c", "space"))
+    placed = P(("x", "z", "c"), "space", None)
     return jax.shard_map(
         shards,
-        mesh=mesh,
+        mesh=split,
         in_specs=(placed,) * 4,
         out_specs=(placed,) * 3,
         check_vma=False,

time: 109 us -> 99.9 us (0.917)
  blocking collectives: 94.9 us -> 46.5 us
  starting transfers between devices: 0 us -> 23.2 us
  waiting for transfers between devices: 0 us -> 16.7 us
    all_to_all x4, blocking collectives: 94.9 us -> 46.5 us  [exchange(): pieces = lax.all_to_all(pieces, ('c', 'space'), 0, 0, tiled=True)]
    ppermute x0 -> x14, starting transfers between devices: none -> 23.2 us  [shift(): lax.ppermute(value, axis, [(i, (i + by) % size) for i in range(size)])]
    ppermute x0 -> x14, waiting for transfers between devices: none -> 16.7 us  [shift(): lax.ppermute(value, axis, [(i, (i + by) % size) for i in range(size)])]
  transfers between devices with their start and end apart: 0 -> 14, of which waited for: 0 -> 11; matrix products, arithmetic and copies ran while one was open for 0% -> 0% of each run, Pallas kernels for 0% -> 0%
where the time goes in v2:
time: 99.9 us; the launch traced here: 99.4 us
  blocking collectives  46.5 us (47%)
  starting transfers between devices  23.2 us (23%)
  waiting for transfers between devices  16.7 us (17%)
  Pallas kernels  9.77 us (10%)
  local copies, waits for them, and re-layouts  2.55 us (3%)
    all_to_all x4, blocking collectives, exchange(): pieces = lax.all_to_all(pieces, ('c', 'space'), 0, 0, tiled=True)  46.5 us
    ppermute x14, starting transfers between devices, shift(): lax.ppermute(value, axis, [(i, (i + by) % size) for i in range(size)])  23.2 us
    ppermute x14, waiting for transfers between devices, shift(): lax.ppermute(value, axis, [(i, (i + by) % size) for i in range(size)])  16.7 us
    pallas_call x1, Pallas kernels, shards(): pl.pallas_call(query_kernel, grid=(STEPS,), in_specs=[rows_spec, rows_spe...  5.23 us
    pallas_call x1, Pallas kernels, shards(): pl.pallas_call(key_kernel, grid=(STEPS,), in_specs=[rows_spec, rows_spec,...  3.07 us
    unnamed x12, local copies, waits for them, and re-layouts  2.55 us
  transfers between devices with their start and end apart: 14, of which 11 were waited for; matrix products, arithmetic and copies ran while one was open for 0% of the time, Pallas kernels for 0%

profile of v2, /device:TPU:1, one launch (start us, length us, event | category | flops | bytes accessed | tf_op | source)
XLA Modules:
  0.0 99.4 jit_solution(5067541316511485602)
XLA Ops:
  0.6 1.3 %copy-done = bf16[1,512,1152]{2,1,0:T(8,128)(2,1)S(1)} copy-done((bf16[1,512,1152]{2,1,0:T(8,128)(2,1)S(1)}, bf16[1,512,1152]{2,1,0:T(8,128)(2,1)}, u32[]{:S(2)}) %copy-start) | copy-done | bytes 1179672
  1.9 1.3 %copy-done.2 = bf16[1,512,1152]{2,1,0:T(8,128)(2,1)S(1)} copy-done((bf16[1,512,1152]{2,1,0:T(8,128)(2,1)S(1)}, bf16[1,512,1152]{2,1,0:T(8,128)(2,1)}, u32[]{:S(2)}) %copy-start.2) | copy-done | bytes 1179672
  3.2 1.3 %blocks.1 = f32[320,128]{1,0:T(8,128)S(1)} custom-call(bf16[1,512,1152]{2,1,0:T(8,128)(2,1)S(1)} %copy-done, bf16[1,512,1152]{2,1,0:T(8,128)(2,1)S(1)} %copy-done.2), custom_call_target="tpu_custom_call" | custom-call | tf_op jit(solution)/shard_map/blocks/pallas_call | solution.py:233
  4.5 11.4 %all_to_all.20 = f32[8,40,128]{2,1,0:T(8,128)S(1)} all-to-all(f32[8,40,128]{2,1,0:T(8,128)S(1)} %bitcast.10), channel_id=1, replica_groups=mesh['x'=4,'z'=8,'c'=2,'space'=4] {'c','space'}, dimensions={0} | all-to-all | bytes 327680 | tf_op jit(solution)/shard_map/all_to_all | solution.py:213
  16.0 5.7 %collective-permute-start.1 = (f32[40,128]{1,0:T(8,128)S(1)}, f32[40,128]{1,0:T(8,128)S(1)}, u32[]{:S(2)}, u32[]{:S(2)}) collective-permute-start(f32[40,128]{1,0:T(8,128)S(1)} %get-tuple-element.19.refs_0_.refs_2_), channel_id=1, source_target_pairs={{0,56},{8,0},{16,8},{24,16},{32,24},{40,32},{48,40},{56,48},{1,57}... | collective-permute-start | bytes 61448 | tf_op jit(solution)/shard_map/ppermute | solution.py:217
  22.5 2.9 %collective-permute-done.refs_1_ = f32[40,128]{1,0:T(8,128)S(1)} collective-permute-done((f32[40,128]{1,0:T(8,128)S(1)}, f32[40,128]{1,0:T(8,128)S(1)}, u32[]{:S(2)}, u32[]{:S(2)}) %collective-permute-start) | collective-permute-done | bytes 20512 | tf_op jit(solution)/shard_map/ppermute | solution.py:217
  25.6 4.5 %collective-permute-start.3 = (f32[80,128]{1,0:T(8,128)S(1)}, f32[80,128]{1,0:T(8,128)S(1)}, u32[]{:S(2)}, u32[]{:S(2)}) collective-permute-start(f32[80,128]{1,0:T(8,128)S(1)} %get-tuple-element.21), channel_id=1, source_target_pairs={{0,40},{8,48},{16,56},{24,0},{32,8},{40,16},{48,24},{56,32},{1,41}... | collective-permute-start | bytes 122888 | tf_op jit(solution)/shard_map/ppermute | solution.py:217
  30.0 1.8 %collective-permute-done.2.refs_3_ = f32[80,128]{1,0:T(8,128)S(1)} collective-permute-done((f32[80,128]{1,0:T(8,128)S(1)}, f32[80,128]{1,0:T(8,128)S(1)}, u32[]{:S(2)}, u32[]{:S(2)}) %collective-permute-start.2) | collective-permute-done | bytes 40992 | tf_op jit(solution)/shard_map/ppermute | solution.py:217
  31.9 2.6 %collective-permute-start.6 = (f32[40,128]{1,0:T(8,128)S(1)}, f32[40,128]{1,0:T(8,128)S(1)}, u32[]{:S(2)}, u32[]{:S(2)}) collective-permute-start(f32[40,128]{1,0:T(8,128)S(1)} %get-tuple-element.24), channel_id=1, source_target_pairs={{0,192},{64,0},{128,64},{192,128},{1,193},{65,1},{129,65},{193,129... | collective-permute-start | bytes 61448 | tf_op jit(solution)/shard_map/ppermute | solution.py:217
  35.6 3.0 %collective-permute-done.5.refs_4_ = f32[40,128]{1,0:T(8,128)S(1)} collective-permute-done((f32[40,128]{1,0:T(8,128)S(1)}, f32[40,128]{1,0:T(8,128)S(1)}, u32[]{:S(2)}, u32[]{:S(2)}) %collective-permute-start.5) | collective-permute-done | bytes 20512 | tf_op jit(solution)/shard_map/ppermute | solution.py:217
  38.8 12.7 %all_to_all.21 = f32[8,40,128]{2,1,0:T(8,128)S(1)} all-to-all(f32[8,40,128]{2,1,0:T(8,128)S(1)} %bitcast.11), channel_id=1, replica_groups=mesh['x'=4,'z'=8,'c'=2,'space'=4] {'c','space'}, dimensions={0} | all-to-all | bytes 327680 | tf_op jit(solution)/shard_map/all_to_all | solution.py:213
  51.5 5.2 %queries.1 = (bf16[1,512,1152]{2,1,0:T(8,128)(2,1)}, f32[320,128]{1,0:T(8,128)S(1)}) custom-call(bf16[1,512,1152]{2,1,0:T(8,128)(2,1)S(1)} %copy-done.4, bf16[1,512,1152]{2,1,0:T(8,128)(2,1)S(1)} %copy-done.5, f32[320,128]{1,0:T(8,128)S(1)} %bitcast.8), custom_call_target="tpu_custom_call" | custom-call | tf_op jit(solution)/shard_map/queries/pallas_call | solution.py:243
  56.8 8.8 %all_to_all.22 = f32[8,40,128]{2,1,0:T(8,128)S(1)} all-to-all(f32[8,40,128]{2,1,0:T(8,128)S(1)} %bitcast.15), channel_id=1, replica_groups=mesh['x'=4,'z'=8,'c'=2,'space'=4] {'c','space'}, dimensions={0} | all-to-all | bytes 327680 | tf_op jit(solution)/shard_map/all_to_all | solution.py:213
  65.7 1.9 %collective-permute-start.7 = (f32[40,128]{1,0:T(8,128)S(1)}, f32[40,128]{1,0:T(8,128)S(1)}, u32[]{:S(2)}, u32[]{:S(2)}) collective-permute-start(f32[40,128]{1,0:T(8,128)S(1)} %get-tuple-element.27.refs_0_.refs_2_), channel_id=1, source_target_pairs={{0,8},{8,16},{16,24},{24,32},{32,40},{40,48},{48,56},{56,0},{1,9},... | collective-permute-start | bytes 61448 | tf_op jit(solution)/shard_map/ppermute | solution.py:217
  67.6 1.1 %collective-permute-done.8.refs_2_ = f32[40,128]{1,0:T(8,128)S(1)} collective-permute-done((f32[40,128]{1,0:T(8,128)S(1)}, f32[40,128]{1,0:T(8,128)S(1)}, u32[]{:S(2)}, u32[]{:S(2)}) %collective-permute-start.8) | collective-permute-done | bytes 20512 | tf_op jit(solution)/shard_map/ppermute | solution.py:217
  69.7 2.6 %collective-permute-start.9 = (f32[80,128]{1,0:T(8,128)S(1)}, f32[80,128]{1,0:T(8,128)S(1)}, u32[]{:S(2)}, u32[]{:S(2)}) collective-permute-start(f32[80,128]{1,0:T(8,128)S(1)} %get-tuple-element.28), channel_id=1, source_target_pairs={{0,24},{8,32},{16,40},{24,48},{32,56},{40,0},{48,8},{56,16},{1,25}... | collective-permute-start | bytes 122888 | tf_op jit(solution)/shard_map/ppermute | solution.py:217
  72.2 2.0 %collective-permute-start.10 = (f32[80,128]{1,0:T(8,128)S(1)}, f32[80,128]{1,0:T(8,128)S(1)}, u32[]{:S(2)}, u32[]{:S(2)}) collective-permute-start(f32[80,128]{1,0:T(8,128)S(1)} %get-tuple-element.29), channel_id=1, source_target_pairs={{0,40},{8,48},{16,56},{24,0},{32,8},{40,16},{48,24},{56,32},{1,41}... | collective-permute-start | bytes 122888 | tf_op jit(solution)/shard_map/ppermute | solution.py:217
  74.2 1.4 %collective-permute-done.9.refs_3_ = f32[80,128]{1,0:T(8,128)S(1)} collective-permute-done((f32[80,128]{1,0:T(8,128)S(1)}, f32[80,128]{1,0:T(8,128)S(1)}, u32[]{:S(2)}, u32[]{:S(2)}) %collective-permute-start.9) | collective-permute-done | bytes 40992 | tf_op jit(solution)/shard_map/ppermute | solution.py:217
  75.6 1.3 %collective-permute-done.10.refs_4_ = f32[80,128]{1,0:T(8,128)S(1)} collective-permute-done((f32[80,128]{1,0:T(8,128)S(1)}, f32[80,128]{1,0:T(8,128)S(1)}, u32[]{:S(2)}, u32[]{:S(2)}) %collective-permute-start.10) | collective-permute-done | bytes 40992 | tf_op jit(solution)/shard_map/ppermute | solution.py:217
  77.6 1.3 %collective-permute-start.12 = (f32[40,128]{1,0:T(8,128)S(1)}, f32[40,128]{1,0:T(8,128)S(1)}, u32[]{:S(2)}, u32[]{:S(2)}) collective-permute-start(f32[40,128]{1,0:T(8,128)S(1)} %get-tuple-element.32), channel_id=1, source_target_pairs={{0,128},{64,192},{128,0},{192,64},{1,129},{65,193},{129,1},{193,65... | collective-permute-start | bytes 61448 | tf_op jit(solution)/shard_map/ppermute | solution.py:217
  79.7 2.1 %collective-permute-done.12.refs_4_ = f32[40,128]{1,0:T(8,128)S(1)} collective-permute-done((f32[40,128]{1,0:T(8,128)S(1)}, f32[40,128]{1,0:T(8,128)S(1)}, u32[]{:S(2)}, u32[]{:S(2)}) %collective-permute-start.12) | collective-permute-done | bytes 20512 | tf_op jit(solution)/shard_map/ppermute | solution.py:217
  81.8 1.0 %collective-permute-done.11.refs_3_ = f32[40,128]{1,0:T(8,128)S(1)} collective-permute-done((f32[40,128]{1,0:T(8,128)S(1)}, f32[40,128]{1,0:T(8,128)S(1)}, u32[]{:S(2)}, u32[]{:S(2)}) %collective-permute-start.11) | collective-permute-done | bytes 20512 | tf_op jit(solution)/shard_map/ppermute | solution.py:217
  82.8 13.5 %all_to_all.23 = f32[8,40,128]{2,1,0:T(8,128)S(1)} all-to-all(f32[8,40,128]{2,1,0:T(8,128)S(1)} %bitcast.12), channel_id=1, replica_groups=mesh['x'=4,'z'=8,'c'=2,'space'=4] {'c','space'}, dimensions={0} | all-to-all | bytes 327680 | tf_op jit(solution)/shard_map/all_to_all | solution.py:213
  96.3 3.1 %keys.1 = (bf16[1,512,1152]{2,1,0:T(8,128)(2,1)}, bf16[1,512,1152]{2,1,0:T(8,128)(2,1)}) custom-call(bf16[1,512,1152]{2,1,0:T(8,128)(2,1)S(1)} %copy-done.1, bf16[1,512,1152]{2,1,0:T(8,128)(2,1)S(1)} %copy-done.3, f32[320,128]{1,0:T(8,128)S(1)} %bitcast.9), custom_call_target="tpu_custom_call" | custom-call | tf_op jit(solution)/shard_map/keys/pallas_call | solution.py:253
  (31 shorter events, 5.0 us)
Async XLA Ops:
  0.6 1.3 %copy-start = (bf16[1,512,1152]{2,1,0:T(8,128)(2,1)S(1)}, bf16[1,512,1152]{2,1,0:T(8,128)(2,1)}, u32[]{:S(2)}) copy-start(bf16[1,512,1152]{2,1,0:T(8,128)(2,1)} %key_ref.3) | copy-start | bytes 3538948
  1.9 1.3 %copy-start.2 = (bf16[1,512,1152]{2,1,0:T(8,128)(2,1)S(1)}, bf16[1,512,1152]{2,1,0:T(8,128)(2,1)}, u32[]{:S(2)}) copy-start(bf16[1,512,1152]{2,1,0:T(8,128)(2,1)} %value_ref.3) | copy-start | bytes 3538948
  3.2 48.4 %copy-start.5 = (bf16[1,512,1152]{2,1,0:T(8,128)(2,1)S(1)}, bf16[1,512,1152]{2,1,0:T(8,128)(2,1)}, u32[]{:S(2)}) copy-start(bf16[1,512,1152]{2,1,0:T(8,128)(2,1)} %grad_ref.1) | copy-start | bytes 3538948
  4.5 47.0 %copy-start.4 = (bf16[1,512,1152]{2,1,0:T(8,128)(2,1)S(1)}, bf16[1,512,1152]{2,1,0:T(8,128)(2,1)}, u32[]{:S(2)}) copy-start(bf16[1,512,1152]{2,1,0:T(8,128)(2,1)} %query_ref.1) | copy-start | bytes 3538948
  16.0 6.6 %collective-permute-start.1 = (f32[40,128]{1,0:T(8,128)S(1)}, f32[40,128]{1,0:T(8,128)S(1)}, u32[]{:S(2)}, u32[]{:S(2)}) collective-permute-start(f32[40,128]{1,0:T(8,128)S(1)} %get-tuple-element.19.refs_0_.refs_2_), channel_id=1, source_target_pairs={{0,56},{8,0},{16,8},{24,16},{32,24},{40,32},{48,40},{56,48},{1,57}... | collective-permute-start | bytes 61448 | tf_op jit(solution)/shard_map/ppermute | solution.py:217
  21.6 3.8 %collective-permute-start = (f32[40,128]{1,0:T(8,128)S(1)}, f32[40,128]{1,0:T(8,128)S(1)}, u32[]{:S(2)}, u32[]{:S(2)}) collective-permute-start(f32[40,128]{1,0:T(8,128)S(1)} %get-tuple-element.19.refs_0_.refs_2_), channel_id=1, source_target_pairs={{0,8},{8,16},{16,24},{24,32},{32,40},{40,48},{48,56},{56,0},{1,9},... | collective-permute-start | bytes 61448 | tf_op jit(solution)/shard_map/ppermute | solution.py:217
  25.5 6.4 %collective-permute-start.2 = (f32[80,128]{1,0:T(8,128)S(1)}, f32[80,128]{1,0:T(8,128)S(1)}, u32[]{:S(2)}, u32[]{:S(2)}) collective-permute-start(f32[80,128]{1,0:T(8,128)S(1)} %get-tuple-element.20), channel_id=1, source_target_pairs={{0,24},{8,32},{16,40},{24,48},{32,56},{40,0},{48,8},{56,16},{1,25}... | collective-permute-start | bytes 122888 | tf_op jit(solution)/shard_map/ppermute | solution.py:217
  25.6 6.3 %collective-permute-start.3 = (f32[80,128]{1,0:T(8,128)S(1)}, f32[80,128]{1,0:T(8,128)S(1)}, u32[]{:S(2)}, u32[]{:S(2)}) collective-permute-start(f32[80,128]{1,0:T(8,128)S(1)} %get-tuple-element.21), channel_id=1, source_target_pairs={{0,40},{8,48},{16,56},{24,0},{32,8},{40,16},{48,24},{56,32},{1,41}... | collective-permute-start | bytes 122888 | tf_op jit(solution)/shard_map/ppermute | solution.py:217
  31.9 3.7 %collective-permute-start.6 = (f32[40,128]{1,0:T(8,128)S(1)}, f32[40,128]{1,0:T(8,128)S(1)}, u32[]{:S(2)}, u32[]{:S(2)}) collective-permute-start(f32[40,128]{1,0:T(8,128)S(1)} %get-tuple-element.24), channel_id=1, source_target_pairs={{0,192},{64,0},{128,64},{192,128},{1,193},{65,1},{129,65},{193,129... | collective-permute-start | bytes 61448 | tf_op jit(solution)/shard_map/ppermute | solution.py:217
  34.4 4.1 %collective-permute-start.5 = (f32[40,128]{1,0:T(8,128)S(1)}, f32[40,128]{1,0:T(8,128)S(1)}, u32[]{:S(2)}, u32[]{:S(2)}) collective-permute-start(f32[40,128]{1,0:T(8,128)S(1)} %get-tuple-element.24), channel_id=1, source_target_pairs={{0,128},{64,192},{128,0},{192,64},{1,129},{65,193},{129,1},{193,65... | collective-permute-start | bytes 61448 | tf_op jit(solution)/shard_map/ppermute | solution.py:217
  35.0 3.8 %collective-permute-start.4 = (f32[40,128]{1,0:T(8,128)S(1)}, f32[40,128]{1,0:T(8,128)S(1)}, u32[]{:S(2)}, u32[]{:S(2)}) collective-permute-start(f32[40,128]{1,0:T(8,128)S(1)} %get-tuple-element.24), channel_id=1, source_target_pairs={{0,64},{64,128},{128,192},{192,0},{1,65},{65,129},{129,193},{193,1... | collective-permute-start | bytes 61448 | tf_op jit(solution)/shard_map/ppermute | solution.py:217
  51.5 44.8 %copy-start.3 = (bf16[1,512,1152]{2,1,0:T(8,128)(2,1)S(1)}, bf16[1,512,1152]{2,1,0:T(8,128)(2,1)}, u32[]{:S(2)}) copy-start(bf16[1,512,1152]{2,1,0:T(8,128)(2,1)} %value_ref.3) | copy-start | bytes 3538948
  56.8 39.6 %copy-start.1 = (bf16[1,512,1152]{2,1,0:T(8,128)(2,1)S(1)}, bf16[1,512,1152]{2,1,0:T(8,128)(2,1)}, u32[]{:S(2)}) copy-start(bf16[1,512,1152]{2,1,0:T(8,128)(2,1)} %key_ref.3) | copy-start | bytes 3538948
  65.6 3.1 %collective-permute-start.8 = (f32[40,128]{1,0:T(8,128)S(1)}, f32[40,128]{1,0:T(8,128)S(1)}, u32[]{:S(2)}, u32[]{:S(2)}) collective-permute-start(f32[40,128]{1,0:T(8,128)S(1)} %get-tuple-element.27.refs_0_.refs_2_), channel_id=1, source_target_pairs={{0,56},{8,0},{16,8},{24,16},{32,24},{40,32},{48,40},{56,48},{1,57}... | collective-permute-start | bytes 61448 | tf_op jit(solution)/shard_map/ppermute | solution.py:217
  65.7 3.9 %collective-permute-start.7 = (f32[40,128]{1,0:T(8,128)S(1)}, f32[40,128]{1,0:T(8,128)S(1)}, u32[]{:S(2)}, u32[]{:S(2)}) collective-permute-start(f32[40,128]{1,0:T(8,128)S(1)} %get-tuple-element.27.refs_0_.refs_2_), channel_id=1, source_target_pairs={{0,8},{8,16},{16,24},{24,32},{32,40},{40,48},{48,56},{56,0},{1,9},... | collective-permute-start | bytes 61448 | tf_op jit(solution)/shard_map/ppermute | solution.py:217
  69.7 5.9 %collective-permute-start.9 = (f32[80,128]{1,0:T(8,128)S(1)}, f32[80,128]{1,0:T(8,128)S(1)}, u32[]{:S(2)}, u32[]{:S(2)}) collective-permute-start(f32[80,128]{1,0:T(8,128)S(1)} %get-tuple-element.28), channel_id=1, source_target_pairs={{0,24},{8,32},{16,40},{24,48},{32,56},{40,0},{48,8},{56,16},{1,25}... | collective-permute-start | bytes 122888 | tf_op jit(solution)/shard_map/ppermute | solution.py:217
  72.2 4.7 %collective-permute-start.10 = (f32[80,128]{1,0:T(8,128)S(1)}, f32[80,128]{1,0:T(8,128)S(1)}, u32[]{:S(2)}, u32[]{:S(2)}) collective-permute-start(f32[80,128]{1,0:T(8,128)S(1)} %get-tuple-element.29), channel_id=1, source_target_pairs={{0,40},{8,48},{16,56},{24,0},{32,8},{40,16},{48,24},{56,32},{1,41}... | collective-permute-start | bytes 122888 | tf_op jit(solution)/shard_map/ppermute | solution.py:217
  76.9 2.8 %collective-permute-start.13 = (f32[40,128]{1,0:T(8,128)S(1)}, f32[40,128]{1,0:T(8,128)S(1)}, u32[]{:S(2)}, u32[]{:S(2)}) collective-permute-start(f32[40,128]{1,0:T(8,128)S(1)} %get-tuple-element.32), channel_id=1, source_target_pairs={{0,192},{64,0},{128,64},{192,128},{1,193},{65,1},{129,65},{193,129... | collective-permute-start | bytes 61448 | tf_op jit(solution)/shard_map/ppermute | solution.py:217
  77.6 4.1 %collective-permute-start.12 = (f32[40,128]{1,0:T(8,128)S(1)}, f32[40,128]{1,0:T(8,128)S(1)}, u32[]{:S(2)}, u32[]{:S(2)}) collective-permute-start(f32[40,128]{1,0:T(8,128)S(1)} %get-tuple-element.32), channel_id=1, source_target_pairs={{0,128},{64,192},{128,0},{192,64},{1,129},{65,193},{129,1},{193,65... | collective-permute-start | bytes 61448 | tf_op jit(solution)/shard_map/ppermute | solution.py:217
  78.9 3.8 %collective-permute-start.11 = (f32[40,128]{1,0:T(8,128)S(1)}, f32[40,128]{1,0:T(8,128)S(1)}, u32[]{:S(2)}, u32[]{:S(2)}) collective-permute-start(f32[40,128]{1,0:T(8,128)S(1)} %get-tuple-element.32), channel_id=1, source_target_pairs={{0,64},{64,128},{128,192},{192,0},{1,65},{65,129},{129,193},{193,1... | collective-permute-start | bytes 61448 | tf_op jit(solution)/shard_map/ppermute | solution.py:217

commit v3 on v1

--- a/solution.py
+++ b/solution.py
@@ -3,6 +3,7 @@
 from jax import lax
 from jax.experimental import pallas as pl
 from jax.experimental.pallas import tpu as pltpu
+from jax.sharding import Mesh
 from jax.sharding import PartitionSpec as P
 
 HEAD_DIM = 32
@@ -11,7 +12,10 @@
 STEPS = 3
 PER_STEP = GROUPS // STEPS
 STATE_ROWS = GROUPS * HEAD_DIM
-ROWS = 512
+X, Z, CORES, SPACE = 4, 8, 2, 4
+CHUNK = 10
+PLANE = X * CHUNK
+ROWS = X * CORES * SPACE * CHUNK
 FRAME_TOK = 2048
 
 ROW_BY_ROW = (((0,), (0,)), ((), ()))
@@ -64,32 +68,54 @@
         )
 
 
-def scan_kernel(backward, sent_ref, out_ref):
-    devices = ROWS // 2
-    row = lax.broadcasted_iota(jnp.int32, (devices, devices), 0) // 4
-    col = lax.broadcasted_iota(jnp.int32, (devices, devices), 1) // 4
-    pick = (col >= row) if backward else (col <= row)
-    pick = jnp.where(pick, 1.0, 0.0).astype(jnp.bfloat16)
-    frame = lax.broadcasted_iota(jnp.int32, (devices, LANES), 0) // 4
-    count = ((frame + 1) * FRAME_TOK).astype(jnp.float32)
-    for half in range(2):
-        rows = pl.ds(half, devices, stride=2)
-        terms = sent_ref[rows, :]
-        if backward:
-            terms = terms / count
-        high = terms.astype(jnp.bfloat16)
-        rest = terms - high.astype(jnp.float32)
-        middle, low = halves(rest)
-        total = dot(pick, low, PLAIN) + dot(pick, middle, PLAIN) + dot(pick, high, PLAIN)
-        if not backward:
-            total = total / count
-        out_ref[rows, :] = total
+def rows_of(x, core, space=0):
+    base = ((x * CORES + core) * SPACE + space) * CHUNK
+    return slice(base, base + CHUNK)
+
+
+def plane_kernel(backward, pieces_ref, out_ref, edge_ref, both_ref, ahead_ref):
+    z = lax.axis_index("z")
+    total = jnp.zeros((CHUNK, LANES), jnp.float32)
+    for x in reversed(range(X)) if backward else range(X):
+        cores = []
+        for core in range(CORES):
+            parts = [pieces_ref[rows_of(x, core, s), :] for s in range(SPACE)]
+            cores.append((parts[0] + parts[1]) + (parts[2] + parts[3]))
+        both = cores[0] + cores[1]
+        rows = slice(x * CHUNK, (x + 1) * CHUNK)
+        edge_ref[rows, :] = cores[1] if backward else cores[0]
+        both_ref[rows, :] = both
+        ahead_ref[rows, :] = total
+        total = total + both
+    ahead, both = ahead_ref[...], both_ref[...]
+    for target in range(Z):
+        comes = (z > target) if backward else (z < target)
+        out_ref[target * PLANE : (target + 1) * PLANE, :] = ahead + jnp.where(comes, both, 0.0)
+
+
+def frame_kernel(backward, lines_ref, edge_ref, both_ref, out_ref, total_ref):
+    z = lax.axis_index("z")
+    lines = [lines_ref[i * PLANE : (i + 1) * PLANE, :] for i in range(Z)]
+    while len(lines) > 1:
+        lines = [first + second for first, second in zip(lines[::2], lines[1::2])]
+    for core in range(CORES):
+        near = both_ref if (core == 0) == backward else edge_ref
+        total_ref[...] = lines[0] + near[...]
+        for x in range(X):
+            frame = total_ref[x * CHUNK : (x + 1) * CHUNK, :]
+            if not backward:
+                count = ((x * Z + z) * CORES + core + 1) * FRAME_TOK
+                frame = frame / count.astype(jnp.float32)
+            for space in range(SPACE):
+                out_ref[rows_of(x, core, space), :] = frame
 
 
 def query_kernel(query_ref, grad_ref, state_ref, out_ref, adj_ref):
     step = pl.program_id(0)
     same = same_head()
     ones = jnp.where(same, 1.0, 0.0).astype(jnp.bfloat16)
+    frame = (lax.axis_index("x") * Z + lax.axis_index("z")) * CORES + lax.axis_index("c")
+    count = ((frame + 1) * FRAME_TOK).astype(jnp.float32)
 
     @pl.when(step == 0)
     def _():
@@ -118,9 +144,9 @@
         ).astype(jnp.bfloat16)
         high, low = halves(grad.astype(jnp.float32) * scale)
         full = dot(feat, low, ROW_BY_ROW) + dot(feat, high, ROW_BY_ROW)
-        adj_ref[pl.ds(group * HEAD_DIM, HEAD_DIM), :] = gather_heads(full, same)
-        adj_ref[pl.ds(STATE_ROWS + group, 1), :] = jnp.sum(
-            grad_denom * feat_wide, axis=0, keepdims=True
+        adj_ref[pl.ds(group * HEAD_DIM, HEAD_DIM), :] = gather_heads(full, same) / count
+        adj_ref[pl.ds(STATE_ROWS + group, 1), :] = (
+            jnp.sum(grad_denom * feat_wide, axis=0, keepdims=True) / count
         )
 
 
@@ -152,18 +178,29 @@
     whole_shape = jax.ShapeDtypeStruct((ROWS, LANES), jnp.float32)
     params = pltpu.CompilerParams(vmem_limit_bytes=32 * 1024 * 1024)
 
-    def exchange(whole):
-        pieces = whole.reshape(ROWS // 2, 2, LANES)
-        pieces = lax.all_to_all(pieces, ("frame", "space"), 0, 0, tiled=True)
-        return pieces.reshape(ROWS, LANES)
+    plane_shape = jax.ShapeDtypeStruct((PLANE, LANES), jnp.float32)
+
+    def small(kernel, backward, name, shapes, *args):
+        return pl.pallas_call(
+            lambda *refs: kernel(backward, *refs),
+            out_shape=shapes,
+            scratch_shapes=[pltpu.VMEM((PLANE, LANES), jnp.float32)],
+            compiler_params=params,
+            name=name + ("_later" if backward else "_earlier"),
+        )(*args)
+
+    def exchange(whole, axes, peers):
+        pieces = whole.reshape(peers, ROWS // peers // 2, 2, LANES)
+        return lax.all_to_all(pieces, axes, 0, 0, tiled=True).reshape(ROWS, LANES)
 
     def scan(whole, backward):
-        return pl.pallas_call(
-            lambda sent_ref, out_ref: scan_kernel(backward, sent_ref, out_ref),
-            out_shape=whole_shape,
-            compiler_params=params,
-            name="later" if backward else "earlier",
-        )(whole)
+        plane = ("x", "c", "space")
+        pieces = exchange(whole, plane, X * CORES * SPACE)
+        shapes = (whole_shape, plane_shape, plane_shape)
+        lines, edge, both = small(plane_kernel, backward, "plane", shapes, pieces)
+        lines = exchange(lines, "z", Z)
+        frames = small(frame_kernel, backward, "frame", whole_shape, lines, edge, both)
+        return exchange(frames, plane, X * CORES * SPACE)
 
     blocks = pl.pallas_call(
         block_kernel,
@@ -174,7 +211,7 @@
         compiler_params=params,
         name="blocks",
     )(keys, values)
-    state = exchange(scan(exchange(blocks), False))
+    state = scan(blocks, False)
     grad_query, adjoint = pl.pallas_call(
         query_kernel,
         grid=(STEPS,),
@@ -184,7 +221,7 @@
         compiler_params=params,
         name="queries",
     )(queries, cotangent, state)
-    later = exchange(scan(exchange(adjoint), True))
+    later = scan(adjoint, True)
     grad_key, grad_value = pl.pallas_call(
         key_kernel,
         grid=(STEPS,),
@@ -198,10 +235,11 @@
 
 
 def solution(mesh):
-    placed = P("frame", "space", None)
+    split = Mesh(mesh.devices.reshape(X, Z, CORES, SPACE), ("x", "z", "c", "space"))
+    placed = P(("x", "z", "c"), "space", None)
     return jax.shard_map(
         shards,
-        mesh=mesh,
+        mesh=split,
         in_specs=(placed,) * 4,
         out_specs=(placed,) * 3,
         check_vma=False,

time: 109 us -> 94.9 us (0.87)
  blocking collectives: 94.9 us -> 81.5 us
    all_to_all x4 -> x6, blocking collectives: 94.9 us -> 81.5 us  [exchange(): return lax.all_to_all(pieces, axes, 0, 0, tiled=True).reshape(ROWS, LANES)]
where the time goes in v3:
time: 94.9 us; the launch traced here: 94.5 us
  blocking collectives  81.5 us (86%)
  Pallas kernels  9.77 us (10%)
  local copies, waits for them, and re-layouts  2.55 us (3%)
    all_to_all x6, blocking collectives, exchange(): return lax.all_to_all(pieces, axes, 0, 0, tiled=True).reshape(ROWS, LANES)  81.5 us
    pallas_call x1, Pallas kernels, shards(): pl.pallas_call(query_kernel, grid=(STEPS,), in_specs=[rows_spec, rows_spe...  5.23 us
    pallas_call x1, Pallas kernels, shards(): pl.pallas_call(key_kernel, grid=(STEPS,), in_specs=[rows_spec, rows_spec,...  3.07 us
    unnamed x12, local copies, waits for them, and re-layouts  2.55 us

profile of v3, /device:TPU:1, one launch (start us, length us, event | category | flops | bytes accessed | tf_op | source)
XLA Modules:
  0.0 94.5 jit_solution(2779888984799109086)
XLA Ops:
  0.6 0.0 copy-start
  0.6 1.3 %copy-done = bf16[1,512,1152]{2,1,0:T(8,128)(2,1)S(1)} copy-done((bf16[1,512,1152]{2,1,0:T(8,128)(2,1)S(1)}, bf16[1,512,1152]{2,1,0:T(8,128)(2,1)}, u32[]{:S(2)}) %copy-start) | copy-done | bytes 1179672
  1.9 0.0 copy-start.2
  1.9 1.3 %copy-done.2 = bf16[1,512,1152]{2,1,0:T(8,128)(2,1)S(1)} copy-done((bf16[1,512,1152]{2,1,0:T(8,128)(2,1)S(1)}, bf16[1,512,1152]{2,1,0:T(8,128)(2,1)}, u32[]{:S(2)}) %copy-start.2) | copy-done | bytes 1179672
  3.2 0.0 copy-start.5
  3.2 1.3 %blocks.1 = f32[320,128]{1,0:T(8,128)S(1)} custom-call(bf16[1,512,1152]{2,1,0:T(8,128)(2,1)S(1)} %copy-done, bf16[1,512,1152]{2,1,0:T(8,128)(2,1)S(1)} %copy-done.2), custom_call_target="tpu_custom_call" | custom-call | tf_op jit(solution)/shard_map/blocks/pallas_call | solution.py:205
  4.5 0.0 copy-start.4
  4.5 16.4 %all_to_all.30 = f32[32,5,2,128]{3,2,1,0:T(2,128)S(1)} all-to-all(f32[32,5,2,128]{3,2,1,0:T(2,128)S(1)} %bitcast.14), channel_id=1, replica_groups=mesh['x'=4,'z'=8,'c'=2,'space'=4] {'x','c','space'}, dimensions={0} | all-to-all | bytes 327680 | tf_op jit(solution)/shard_map/all_to_all | solution.py:194
  21.0 16.4 %all_to_all.31 = f32[8,20,2,128]{3,2,1,0:T(2,128)S(1)} all-to-all(f32[8,20,2,128]{3,2,1,0:T(2,128)S(1)} %bitcast.21), channel_id=1, replica_groups=mesh['x'=4,'z'=8,'c'=2,'space'=4] {'z'}, dimensions={0} | all-to-all | bytes 327680 | tf_op jit(solution)/shard_map/all_to_all | solution.py:194
  37.4 13.1 %all_to_all.32 = f32[32,5,2,128]{3,2,1,0:T(2,128)S(1)} all-to-all(f32[32,5,2,128]{3,2,1,0:T(2,128)S(1)} %bitcast.19), channel_id=1, replica_groups=mesh['x'=4,'z'=8,'c'=2,'space'=4] {'x','c','space'}, dimensions={0} | all-to-all | bytes 327680 | tf_op jit(solution)/shard_map/all_to_all | solution.py:194
  50.5 0.0 copy-done.5
  50.5 0.0 copy-done.4
  50.5 0.0 copy-start.3
  50.5 5.2 %queries.1 = (bf16[1,512,1152]{2,1,0:T(8,128)(2,1)}, f32[320,128]{1,0:T(8,128)S(1)}) custom-call(bf16[1,512,1152]{2,1,0:T(8,128)(2,1)S(1)} %copy-done.4, bf16[1,512,1152]{2,1,0:T(8,128)(2,1)S(1)} %copy-done.5, f32[320,128]{1,0:T(8,128)S(1)} %bitcast.12), custom_call_target="tpu_custom_call" | custom-call | tf_op jit(solution)/shard_map/queries/pallas_call | solution.py:215
  55.7 0.0 copy-start.1
  55.7 11.9 %all_to_all.33 = f32[32,5,2,128]{3,2,1,0:T(2,128)S(1)} all-to-all(f32[32,5,2,128]{3,2,1,0:T(2,128)S(1)} %bitcast.23), channel_id=1, replica_groups=mesh['x'=4,'z'=8,'c'=2,'space'=4] {'x','c','space'}, dimensions={0} | all-to-all | bytes 327680 | tf_op jit(solution)/shard_map/all_to_all | solution.py:194
  67.6 11.3 %all_to_all.34 = f32[8,20,2,128]{3,2,1,0:T(2,128)S(1)} all-to-all(f32[8,20,2,128]{3,2,1,0:T(2,128)S(1)} %bitcast.22), channel_id=1, replica_groups=mesh['x'=4,'z'=8,'c'=2,'space'=4] {'z'}, dimensions={0} | all-to-all | bytes 327680 | tf_op jit(solution)/shard_map/all_to_all | solution.py:194
  78.9 12.5 %all_to_all.35 = f32[32,5,2,128]{3,2,1,0:T(2,128)S(1)} all-to-all(f32[32,5,2,128]{3,2,1,0:T(2,128)S(1)} %bitcast.20), channel_id=1, replica_groups=mesh['x'=4,'z'=8,'c'=2,'space'=4] {'x','c','space'}, dimensions={0} | all-to-all | bytes 327680 | tf_op jit(solution)/shard_map/all_to_all | solution.py:194
  91.5 0.0 copy-done.3
  91.5 0.0 copy-done.1
  91.5 3.1 %keys.1 = (bf16[1,512,1152]{2,1,0:T(8,128)(2,1)}, bf16[1,512,1152]{2,1,0:T(8,128)(2,1)}) custom-call(bf16[1,512,1152]{2,1,0:T(8,128)(2,1)S(1)} %copy-done.1, bf16[1,512,1152]{2,1,0:T(8,128)(2,1)S(1)} %copy-done.3, f32[320,128]{1,0:T(8,128)S(1)} %bitcast.13), custom_call_target="tpu_custom_call" | custom-call | tf_op jit(solution)/shard_map/keys/pallas_call | solution.py:225
  (4 shorter events, 0.1 us)
Async XLA Ops:
  0.6 1.3 %copy-start = (bf16[1,512,1152]{2,1,0:T(8,128)(2,1)S(1)}, bf16[1,512,1152]{2,1,0:T(8,128)(2,1)}, u32[]{:S(2)}) copy-start(bf16[1,512,1152]{2,1,0:T(8,128)(2,1)} %key_ref.3) | copy-start | bytes 3538948
  1.9 1.3 %copy-start.2 = (bf16[1,512,1152]{2,1,0:T(8,128)(2,1)S(1)}, bf16[1,512,1152]{2,1,0:T(8,128)(2,1)}, u32[]{:S(2)}) copy-start(bf16[1,512,1152]{2,1,0:T(8,128)(2,1)} %value_ref.3) | copy-start | bytes 3538948
  3.2 47.3 %copy-start.5 = (bf16[1,512,1152]{2,1,0:T(8,128)(2,1)S(1)}, bf16[1,512,1152]{2,1,0:T(8,128)(2,1)}, u32[]{:S(2)}) copy-start(bf16[1,512,1152]{2,1,0:T(8,128)(2,1)} %grad_ref.1) | copy-start | bytes 3538948
  4.5 45.9 %copy-start.4 = (bf16[1,512,1152]{2,1,0:T(8,128)(2,1)S(1)}, bf16[1,512,1152]{2,1,0:T(8,128)(2,1)}, u32[]{:S(2)}) copy-start(bf16[1,512,1152]{2,1,0:T(8,128)(2,1)} %query_ref.1) | copy-start | bytes 3538948
  50.5 41.0 %copy-start.3 = (bf16[1,512,1152]{2,1,0:T(8,128)(2,1)S(1)}, bf16[1,512,1152]{2,1,0:T(8,128)(2,1)}, u32[]{:S(2)}) copy-start(bf16[1,512,1152]{2,1,0:T(8,128)(2,1)} %value_ref.3) | copy-start | bytes 3538948
  55.7 35.8 %copy-start.1 = (bf16[1,512,1152]{2,1,0:T(8,128)(2,1)S(1)}, bf16[1,512,1152]{2,1,0:T(8,128)(2,1)}, u32[]{:S(2)}) copy-start(bf16[1,512,1152]{2,1,0:T(8,128)(2,1)} %key_ref.3) | copy-start | bytes 3538948

commit v4 on v3

v4 whole, which is shorter than its diff:
```python
import jax
import jax.numpy as jnp
from jax import lax
from jax.experimental import pallas as pl
from jax.experimental.pallas import tpu as pltpu
from jax.sharding import Mesh
from jax.sharding import PartitionSpec as P

HEAD_DIM = 32
LANES = 128
GROUPS = 9
STATE_ROWS = GROUPS * HEAD_DIM
X, Z, CORES, SPACE = 4, 8, 2, 4
CHUNK = 10
PLANE = X * CHUNK
ROWS = X * CORES * SPACE * CHUNK
FRAME_TOK = 2048
BYTES = 1 << 20

ROW_BY_ROW = (((0,), (0,)), ((), ()))
LANE_BY_LANE = (((1,), (1,)), ((), ()))
PLAIN = (((1,), (0,)), ((), ()))


def dot(lhs, rhs, dims):
    return lax.dot_general(lhs, rhs, dims, preferred_element_type=jnp.float32)


def halves(wide):
    high = wide.astype(jnp.bfloat16)
    low = (wide - high.astype(jnp.float32)).astype(jnp.bfloat16)
    return high, low


def same_head():
    row = lax.broadcasted_iota(jnp.int32, (LANES, LANES), 0)
    lane = lax.broadcasted_iota(jnp.int32, (LANES, LANES), 1)
    return (row // HEAD_DIM) == (lane // HEAD_DIM)


def spread(compact, same):
    return jnp.where(same, jnp.concatenate([compact] * (LANES // HEAD_DIM), axis=0), 0.0)


def gather_heads(full, same):
    full = jnp.where(same, full, 0.0)
    parts = [full[h * HEAD_DIM : (h + 1) * HEAD_DIM] for h in range(LANES // HEAD_DIM)]
    return (parts[0] + parts[1]) + (parts[2] + parts[3])


def twice(narrow):
    return jnp.concatenate([narrow, narrow], axis=1)


def lanes_of(group):
    return slice(group * LANES, (group + 1) * LANES)


def state_of(group):
    return slice(group * HEAD_DIM, (group + 1) * HEAD_DIM)


def norm_of(group):
    return slice(STATE_ROWS + group, STATE_ROWS + group + 1)


def clear_tail(ref):
    ref[STATE_ROWS:, :] = jnp.zeros((ROWS - STATE_ROWS, LANES), jnp.float32)


def block_kernel(key_hbm, value_hbm, out_ref, key_ref, value_ref, sem):
    same = same_head()
    half = key_ref.shape[1] // 2
    pieces = [slice(0, half), slice(half, 2 * half)]
    copies = []
    for i, rows in enumerate(pieces):
        for j, (source, target) in enumerate(((key_hbm, key_ref), (value_hbm, value_ref))):
            copy = pltpu.make_async_copy(source.at[:, rows], target.at[:, rows], sem.at[2 * i + j])
            copy.start()
            copies.append(copy)
    clear_tail(out_ref)
    for i, rows in enumerate(pieces):
        copies[2 * i].wait()
        copies[2 * i + 1].wait()
        for group in range(GROUPS):
            feat = jnp.maximum(key_ref[0, rows, lanes_of(group)], 0)
            full = dot(feat, value_ref[0, rows, lanes_of(group)], ROW_BY_ROW)
            state = gather_heads(full, same)
            norm = jnp.sum(feat.astype(jnp.float32), axis=0, keepdims=True)
            if i:
                state = state + out_ref[state_of(group), :]
                norm = norm + out_ref[norm_of(group), :]
            out_ref[state_of(group), :] = state
            out_ref[norm_of(group), :] = norm


def rows_of(x, core, space=0):
    base = ((x * CORES + core) * SPACE + space) * CHUNK
    return slice(base, base + CHUNK)


def plane_kernel(backward, pieces_ref, out_ref, edge_ref, both_ref, ahead_ref):
    z = lax.axis_index("z")
    total = jnp.zeros((CHUNK, LANES), jnp.float32)
    for x in reversed(range(X)) if backward else range(X):
        cores = []
        for core in range(CORES):
            parts = [pieces_ref[rows_of(x, core, s), :] for s in range(SPACE)]
            cores.append((parts[0] + parts[1]) + (parts[2] + parts[3]))
        both = cores[0] + cores[1]
        rows = slice(x * CHUNK, (x + 1) * CHUNK)
        edge_ref[rows, :] = cores[1] if backward else cores[0]
        both_ref[rows, :] = both
        ahead_ref[rows, :] = total
        total = total + both
    ahead, both = ahead_ref[...], both_ref[...]
    for target in range(Z):
        comes = (z > target) if backward else (z < target)
        out_ref[target * PLANE : (target + 1) * PLANE, :] = ahead + jnp.where(comes, both, 0.0)


def frame_kernel(backward, lines_ref, edge_ref, both_ref, out_ref, total_ref):
    z = lax.axis_index("z")
    lines = [lines_ref[i * PLANE : (i + 1) * PLANE, :] for i in range(Z)]
    while len(lines) > 1:
        lines = [first + second for first, second in zip(lines[::2], lines[1::2])]
    for core in range(CORES):
        near = both_ref if (core == 0) == backward else edge_ref
        total_ref[...] = lines[0] + near[...]
        for x in range(X):
            frame = total_ref[x * CHUNK : (x + 1) * CHUNK, :]
            if not backward:
                count = ((x * Z + z) * CORES + core + 1) * FRAME_TOK
                frame = frame / count.astype(jnp.float32)
            for space in range(SPACE):
                out_ref[rows_of(x, core, space), :] = frame


def query_kernel(query_ref, grad_ref, state_ref, out_ref, adj_ref):
    same = same_head()
    ones = jnp.where(same, 1.0, 0.0).astype(jnp.bfloat16)
    ones = jnp.concatenate([ones, ones], axis=0)
    frame = (lax.axis_index("x") * Z + lax.axis_index("z")) * CORES + lax.axis_index("c")
    count = ((frame + 1) * FRAME_TOK).astype(jnp.float32)
    clear_tail(adj_ref)

    def project(group):
        feat = jnp.maximum(query_ref[0, :, lanes_of(group)], 0)
        grad = grad_ref[0, :, lanes_of(group)]
        state = spread(state_ref[state_of(group), :], same)
        norm = jnp.where(same, state_ref[norm_of(group), :], 0.0)
        denom = dot(twice(feat), jnp.concatenate(halves(norm), axis=1), LANE_BY_LANE) + 1.0
        back = dot(twice(grad), jnp.concatenate(halves(state), axis=1), LANE_BY_LANE)
        return denom, back

    def finish(group, denom, back):
        feat = jnp.maximum(query_ref[0, :, lanes_of(group)], 0)
        grad = grad_ref[0, :, lanes_of(group)].astype(jnp.float32)
        wide = feat.astype(jnp.float32)
        scale = 1.0 / denom
        along = dot(jnp.concatenate(halves(wide * back), axis=1), ones, PLAIN)
        pull = along * scale
        grad_feat = scale * (back - pull * state_ref[norm_of(group), :])
        out_ref[0, :, lanes_of(group)] = jnp.where(wide > 0, grad_feat, 0.0).astype(jnp.bfloat16)
        full = dot(feat, jnp.concatenate(halves(grad * scale), axis=1), ROW_BY_ROW)
        full = full[:, :LANES] + full[:, LANES:]
        adj_ref[state_of(group), :] = gather_heads(full, same) / count
        norm = jnp.sum(pull * scale * wide, axis=0, keepdims=True)
        adj_ref[norm_of(group), :] = -norm / count

    ahead = project(0)
    for group in range(GROUPS):
        ready = ahead
        if group + 1 < GROUPS:
            ahead = project(group + 1)
        finish(group, *ready)


def key_kernel(key_ref, value_ref, state_ref, grad_key_out, grad_value_out, grad_key, grad_value, sem):
    same = same_head()
    copies = []
    for group in range(GROUPS):
        lanes = lanes_of(group)
        high, low = halves(spread(state_ref[state_of(group), :], same))
        key = key_ref[0, :, lanes]
        feat = jnp.maximum(key, 0)
        grad_feat = dot(
            twice(value_ref[0, :, lanes]), jnp.concatenate([high, low], axis=1), LANE_BY_LANE
        )
        grad_feat = grad_feat + state_ref[norm_of(group), :]
        grad_key[0, :, lanes] = jnp.where(key.astype(jnp.float32) > 0, grad_feat, 0.0).astype(
            jnp.bfloat16
        )
        grad_value[0, :, lanes] = dot(
            twice(feat), jnp.concatenate([high, low], axis=0), PLAIN
        ).astype(jnp.bfloat16)
        pairs = ((grad_key, grad_key_out), (grad_value, grad_value_out))
        for j, (source, target) in enumerate(pairs):
            copy = pltpu.make_async_copy(
                source.at[:, :, lanes], target.at[:, :, lanes], sem.at[2 * group + j]
            )
            copy.start()
            copies.append(copy)
    for copy in copies:
        copy.wait()


def shards(queries, keys, values, cotangent):
    vmem = pl.BlockSpec(memory_space=pltpu.VMEM)
    hbm = pl.BlockSpec(memory_space=pl.ANY)
    rows_shape = jax.ShapeDtypeStruct(queries.shape, jnp.bfloat16)
    rows_scratch = pltpu.VMEM(queries.shape, jnp.bfloat16)
    whole_shape = jax.ShapeDtypeStruct((ROWS, LANES), jnp.float32)
    params = pltpu.CompilerParams(vmem_limit_bytes=32 * BYTES)
    plane_shape = jax.ShapeDtypeStruct((PLANE, LANES), jnp.float32)

    def small(kernel, backward, name, shapes, *args):
        return pl.pallas_call(
            lambda *refs: kernel(backward, *refs),
            out_shape=shapes,
            scratch_shapes=[pltpu.VMEM((PLANE, LANES), jnp.float32)],
            compiler_params=params,
            name=name + ("_later" if backward else "_earlier"),
        )(*args)

    def exchange(whole, axes, peers):
        pieces = whole.reshape(peers, ROWS // peers // 2, 2, LANES)
        return lax.all_to_all(pieces, axes, 0, 0, tiled=True).reshape(ROWS, LANES)

    def scan(whole, backward):
        plane = ("x", "c", "space")
        pieces = exchange(whole, plane, X * CORES * SPACE)
        shapes = (whole_shape, plane_shape, plane_shape)
        lines, edge, both = small(plane_kernel, backward, "plane", shapes, pieces)
        lines = exchange(lines, "z", Z)
        frames = small(frame_kernel, backward, "frame", whole_shape, lines, edge, both)
        return exchange(frames, plane, X * CORES * SPACE)

    blocks = pl.pallas_call(
        block_kernel,
        in_specs=[hbm, hbm],
        out_specs=vmem,
        out_shape=whole_shape,
        scratch_shapes=[rows_scratch, rows_scratch, pltpu.SemaphoreType.DMA((4,))],
        compiler_params=pltpu.CompilerParams(vmem_limit_bytes=60 * BYTES),
        name="blocks",
    )(keys, values)
    state = scan(blocks, False)
    grad_query, adjoint = pl.pallas_call(
        query_kernel,
        in_specs=[vmem] * 3,
        out_specs=(vmem, vmem),
        out_shape=(rows_shape, whole_shape),
        compiler_params=params,
        name="queries",
    )(queries, cotangent, state)
    later = scan(adjoint, True)
    grad_key, grad_value = pl.pallas_call(
        key_kernel,
        in_specs=[vmem] * 3,
        out_specs=(hbm, hbm),
        out_shape=(rows_shape, rows_shape),
        scratch_shapes=[rows_scratch, rows_scratch, pltpu.SemaphoreType.DMA((2 * GROUPS,))],
        compiler_params=params,
        name="keys",
    )(keys, values, later)
    return (grad_query, grad_key, grad_value)


def solution(mesh):
    split = Mesh(mesh.devices.reshape(X, Z, CORES, SPACE), ("x", "z", "c", "space"))
    placed = P(("x", "z", "c"), "space", None)
    return jax.shard_map(
        shards,
        mesh=split,
        in_specs=(placed,) * 4,
        out_specs=(placed,) * 3,
        check_vma=False,
    )
```

time: 94.9 us -> 91.5 us (0.964)
  local copies, waits for them, and re-layouts: 2.55 us -> 0.02 us
  Pallas kernels: 9.77 us -> 8.69 us
    unnamed x12 -> x8, local copies, waits for them, and re-layouts: 2.55 us -> 0.02 us
    pallas_call x3, Pallas kernels: 9.62 us -> 8.54 us  [the longest x1 3.52 us: shards(): pl.pallas_call(query_kernel, in_specs=[vmem] * 3, out_specs=(vmem, vmem),...]
where the time goes in v4:
time: 91.5 us; the launch traced here: 91.1 us
  blocking collectives  81.8 us (89%)
  Pallas kernels  8.69 us (9%)
    all_to_all x6, blocking collectives, exchange(): return lax.all_to_all(pieces, axes, 0, 0, tiled=True).reshape(ROWS, LANES)  81.8 us
    pallas_call x1, Pallas kernels, shards(): pl.pallas_call(query_kernel, in_specs=[vmem] * 3, out_specs=(vmem, vmem),...  3.52 us
    pallas_call x1, Pallas kernels, shards(): pl.pallas_call(block_kernel, in_specs=[hbm, hbm], out_specs=vmem, out_sha...  2.75 us
    pallas_call x1, Pallas kernels, shards(): pl.pallas_call(key_kernel, in_specs=[vmem] * 3, out_specs=(hbm, hbm), out...  2.27 us

profile of v4, /device:TPU:1, one launch (start us, length us, event | category | flops | bytes accessed | tf_op | source)
XLA Modules:
  0.0 91.1 jit_solution(1070170205626301540)
XLA Ops:
  0.6 0.0 copy-start.3
  0.6 2.8 %blocks.1 = f32[320,128]{1,0:T(8,128)} custom-call(bf16[1,512,1152]{2,1,0:T(8,128)(2,1)} %key_ref.1, bf16[1,512,1152]{2,1,0:T(8,128)(2,1)} %value_ref.1), custom_call_target="tpu_custom_call" | custom-call | tf_op jit(solution)/shard_map/blocks/pallas_call | solution.py:239
  3.4 0.0 copy-start.2
  3.4 16.6 %all_to_all.30 = f32[32,5,2,128]{3,2,1,0:T(2,128)S(1)} all-to-all(f32[32,5,2,128]{3,2,1,0:T(2,128)} %bitcast.23), channel_id=1, replica_groups=mesh['x'=4,'z'=8,'c'=2,'space'=4] {'x','c','space'}, dimensions={0} | all-to-all | bytes 327680 | tf_op jit(solution)/shard_map/all_to_all | solution.py:228
  20.1 16.4 %all_to_all.31 = f32[8,20,2,128]{3,2,1,0:T(2,128)S(1)} all-to-all(f32[8,20,2,128]{3,2,1,0:T(2,128)S(1)} %bitcast.20), channel_id=1, replica_groups=mesh['x'=4,'z'=8,'c'=2,'space'=4] {'z'}, dimensions={0} | all-to-all | bytes 327680 | tf_op jit(solution)/shard_map/all_to_all | solution.py:228
  36.5 13.1 %all_to_all.32 = f32[32,5,2,128]{3,2,1,0:T(2,128)S(1)} all-to-all(f32[32,5,2,128]{3,2,1,0:T(2,128)S(1)} %bitcast.18), channel_id=1, replica_groups=mesh['x'=4,'z'=8,'c'=2,'space'=4] {'x','c','space'}, dimensions={0} | all-to-all | bytes 327680 | tf_op jit(solution)/shard_map/all_to_all | solution.py:228
  49.6 0.0 copy-done.3
  49.6 0.0 copy-done.2
  49.6 0.0 copy-start.1
  49.6 3.5 %queries.1 = (bf16[1,512,1152]{2,1,0:T(8,128)(2,1)}, f32[320,128]{1,0:T(8,128)S(1)}) custom-call(bf16[1,512,1152]{2,1,0:T(8,128)(2,1)S(1)} %copy-done.2, bf16[1,512,1152]{2,1,0:T(8,128)(2,1)S(1)} %copy-done.3, f32[320,128]{1,0:T(8,128)S(1)} %bitcast.12), custom_call_target="tpu_custom_call" | custom-call | tf_op jit(solution)/shard_map/queries/pallas_call | solution.py:249
  53.1 0.0 copy-start
  53.1 11.9 %all_to_all.33 = f32[32,5,2,128]{3,2,1,0:T(2,128)S(1)} all-to-all(f32[32,5,2,128]{3,2,1,0:T(2,128)S(1)} %bitcast.22), channel_id=1, replica_groups=mesh['x'=4,'z'=8,'c'=2,'space'=4] {'x','c','space'}, dimensions={0} | all-to-all | bytes 327680 | tf_op jit(solution)/shard_map/all_to_all | solution.py:228
  65.0 11.3 %all_to_all.34 = f32[8,20,2,128]{3,2,1,0:T(2,128)S(1)} all-to-all(f32[8,20,2,128]{3,2,1,0:T(2,128)S(1)} %bitcast.21), channel_id=1, replica_groups=mesh['x'=4,'z'=8,'c'=2,'space'=4] {'z'}, dimensions={0} | all-to-all | bytes 327680 | tf_op jit(solution)/shard_map/all_to_all | solution.py:228
  76.3 12.5 %all_to_all.35 = f32[32,5,2,128]{3,2,1,0:T(2,128)S(1)} all-to-all(f32[32,5,2,128]{3,2,1,0:T(2,128)S(1)} %bitcast.19), channel_id=1, replica_groups=mesh['x'=4,'z'=8,'c'=2,'space'=4] {'x','c','space'}, dimensions={0} | all-to-all | bytes 327680 | tf_op jit(solution)/shard_map/all_to_all | solution.py:228
  88.9 0.0 copy-done.1
  88.9 0.0 copy-done
  88.9 2.3 %keys.1 = (bf16[1,512,1152]{2,1,0:T(8,128)(2,1)}, bf16[1,512,1152]{2,1,0:T(8,128)(2,1)}) custom-call(bf16[1,512,1152]{2,1,0:T(8,128)(2,1)S(1)} %copy-done, bf16[1,512,1152]{2,1,0:T(8,128)(2,1)S(1)} %copy-done.1, f32[320,128]{1,0:T(8,128)S(1)} %bitcast.13), custom_call_target="tpu_custom_call" | custom-call | tf_op jit(solution)/shard_map/keys/pallas_call | solution.py:258
  (4 shorter events, 0.1 us)
Async XLA Ops:
  0.6 48.9 %copy-start.3 = (bf16[1,512,1152]{2,1,0:T(8,128)(2,1)S(1)}, bf16[1,512,1152]{2,1,0:T(8,128)(2,1)}, u32[]{:S(2)}) copy-start(bf16[1,512,1152]{2,1,0:T(8,128)(2,1)} %grad_ref.1) | copy-start | bytes 3538948
  3.4 46.2 %copy-start.2 = (bf16[1,512,1152]{2,1,0:T(8,128)(2,1)S(1)}, bf16[1,512,1152]{2,1,0:T(8,128)(2,1)}, u32[]{:S(2)}) copy-start(bf16[1,512,1152]{2,1,0:T(8,128)(2,1)} %query_ref.1) | copy-start | bytes 3538948
  49.6 39.3 %copy-start.1 = (bf16[1,512,1152]{2,1,0:T(8,128)(2,1)S(1)}, bf16[1,512,1152]{2,1,0:T(8,128)(2,1)}, u32[]{:S(2)}) copy-start(bf16[1,512,1152]{2,1,0:T(8,128)(2,1)} %value_ref.1) | copy-start | bytes 3538948
  53.1 35.8 %copy-start = (bf16[1,512,1152]{2,1,0:T(8,128)(2,1)S(1)}, bf16[1,512,1152]{2,1,0:T(8,128)(2,1)}, u32[]{:S(2)}) copy-start(bf16[1,512,1152]{2,1,0:T(8,128)(2,1)} %key_ref.1) | copy-start | bytes 3538948

commit v5 on v4

--- a/solution.py
+++ b/solution.py
@@ -15,6 +15,7 @@
 PLANE = X * CHUNK
 ROWS = X * CORES * SPACE * CHUNK
 FRAME_TOK = 2048
+ENDS = {3: 0, 7: 4, 8: 8}
 BYTES = 1 << 20
 
 ROW_BY_ROW = (((0,), (0,)), ((), ()))
@@ -54,6 +55,10 @@
 
 def lanes_of(group):
     return slice(group * LANES, (group + 1) * LANES)
+
+
+def pair_of(group):
+    return slice(2 * group * LANES, 2 * (group + 1) * LANES)
 
 
 def state_of(group):
@@ -136,13 +141,14 @@
                 out_ref[rows_of(x, core, space), :] = frame
 
 
-def query_kernel(query_ref, grad_ref, state_ref, out_ref, adj_ref):
+def query_kernel(query_ref, grad_ref, state_ref, out_hbm, adj_ref, out_ref, pair_ref, sem):
     same = same_head()
     ones = jnp.where(same, 1.0, 0.0).astype(jnp.bfloat16)
     ones = jnp.concatenate([ones, ones], axis=0)
     frame = (lax.axis_index("x") * Z + lax.axis_index("z")) * CORES + lax.axis_index("c")
     count = ((frame + 1) * FRAME_TOK).astype(jnp.float32)
     clear_tail(adj_ref)
+    copies = []
 
     def project(group):
         feat = jnp.maximum(query_ref[0, :, lanes_of(group)], 0)
@@ -162,9 +168,14 @@
         pull = along * scale
         grad_feat = scale * (back - pull * state_ref[norm_of(group), :])
         out_ref[0, :, lanes_of(group)] = jnp.where(wide > 0, grad_feat, 0.0).astype(jnp.bfloat16)
-        full = dot(feat, jnp.concatenate(halves(grad * scale), axis=1), ROW_BY_ROW)
-        full = full[:, :LANES] + full[:, LANES:]
-        adj_ref[state_of(group), :] = gather_heads(full, same) / count
+        if group in ENDS:
+            lanes = slice(ENDS[group] * LANES, (group + 1) * LANES)
+            copy = pltpu.make_async_copy(
+                out_ref.at[:, :, lanes], out_hbm.at[:, :, lanes], sem.at[len(copies)]
+            )
+            copy.start()
+            copies.append(copy)
+        pair_ref[:, pair_of(group)] = jnp.concatenate(halves(grad * scale), axis=1)
         norm = jnp.sum(pull * scale * wide, axis=0, keepdims=True)
         adj_ref[norm_of(group), :] = -norm / count
 
@@ -174,6 +185,13 @@
         if group + 1 < GROUPS:
             ahead = project(group + 1)
         finish(group, *ready)
+    for group in range(GROUPS):
+        feat = jnp.maximum(query_ref[0, :, lanes_of(group)], 0)
+        full = dot(feat, pair_ref[:, pair_of(group)], ROW_BY_ROW)
+        full = full[:, :LANES] + full[:, LANES:]
+        adj_ref[state_of(group), :] = gather_heads(full, same) / count
+    for copy in copies:
+        copy.wait()
 
 
 def key_kernel(key_ref, value_ref, state_ref, grad_key_out, grad_value_out, grad_key, grad_value, sem):
@@ -249,8 +267,13 @@
     grad_query, adjoint = pl.pallas_call(
         query_kernel,
         in_specs=[vmem] * 3,
-        out_specs=(vmem, vmem),
+        out_specs=(hbm, vmem),
         out_shape=(rows_shape, whole_shape),
+        scratch_shapes=[
+            rows_scratch,
+            pltpu.VMEM((queries.shape[1], 2 * queries.shape[2]), jnp.bfloat16),
+            pltpu.SemaphoreType.DMA((len(ENDS),)),
+        ],
         compiler_params=params,
         name="queries",
     )(queries, cotangent, state)

time: 91.5 us -> 91 us (level)
  no operation moved by 1% of the time
where the time goes in v5:
time: 91 us; the launch traced here: 90.7 us
  blocking collectives  81.8 us (90%)
  Pallas kernels  8.18 us (9%)
    all_to_all x6, blocking collectives, exchange(): return lax.all_to_all(pieces, axes, 0, 0, tiled=True).reshape(ROWS, LANES)  81.8 us
    pallas_call x1, Pallas kernels, shards(): pl.pallas_call(query_kernel, in_specs=[vmem] * 3, out_specs=(hbm, vmem),...  3.01 us
    pallas_call x1, Pallas kernels, shards(): pl.pallas_call(block_kernel, in_specs=[hbm, hbm], out_specs=vmem, out_sha...  2.75 us
    pallas_call x1, Pallas kernels, shards(): pl.pallas_call(key_kernel, in_specs=[vmem] * 3, out_specs=(hbm, hbm), out...  2.27 us

profile of v5, /device:TPU:1, one launch (start us, length us, event | category | flops | bytes accessed | tf_op | source)
XLA Modules:
  0.0 90.7 jit_solution(5326698013801147810)
XLA Ops:
  0.6 0.0 copy-start.3
  0.6 2.8 %blocks.1 = f32[320,128]{1,0:T(8,128)} custom-call(bf16[1,512,1152]{2,1,0:T(8,128)(2,1)} %key_ref.1, bf16[1,512,1152]{2,1,0:T(8,128)(2,1)} %value_ref.1), custom_call_target="tpu_custom_call" | custom-call | tf_op jit(solution)/shard_map/blocks/pallas_call | solution.py:257
  3.4 0.0 copy-start.2
  3.4 16.6 %all_to_all.30 = f32[32,5,2,128]{3,2,1,0:T(2,128)S(1)} all-to-all(f32[32,5,2,128]{3,2,1,0:T(2,128)} %bitcast.23), channel_id=1, replica_groups=mesh['x'=4,'z'=8,'c'=2,'space'=4] {'x','c','space'}, dimensions={0} | all-to-all | bytes 327680 | tf_op jit(solution)/shard_map/all_to_all | solution.py:246
  20.1 16.4 %all_to_all.31 = f32[8,20,2,128]{3,2,1,0:T(2,128)S(1)} all-to-all(f32[8,20,2,128]{3,2,1,0:T(2,128)S(1)} %bitcast.20), channel_id=1, replica_groups=mesh['x'=4,'z'=8,'c'=2,'space'=4] {'z'}, dimensions={0} | all-to-all | bytes 327680 | tf_op jit(solution)/shard_map/all_to_all | solution.py:246
  36.5 13.1 %all_to_all.32 = f32[32,5,2,128]{3,2,1,0:T(2,128)S(1)} all-to-all(f32[32,5,2,128]{3,2,1,0:T(2,128)S(1)} %bitcast.18), channel_id=1, replica_groups=mesh['x'=4,'z'=8,'c'=2,'space'=4] {'x','c','space'}, dimensions={0} | all-to-all | bytes 327680 | tf_op jit(solution)/shard_map/all_to_all | solution.py:246
  49.6 0.0 copy-done.3
  49.6 0.0 copy-done.2
  49.6 0.0 copy-start.1
  49.6 3.0 %queries.1 = (bf16[1,512,1152]{2,1,0:T(8,128)(2,1)}, f32[320,128]{1,0:T(8,128)S(1)}) custom-call(bf16[1,512,1152]{2,1,0:T(8,128)(2,1)S(1)} %copy-done.2, bf16[1,512,1152]{2,1,0:T(8,128)(2,1)S(1)} %copy-done.3, f32[320,128]{1,0:T(8,128)S(1)} %bitcast.12), custom_call_target="tpu_custom_call" | custom-call | tf_op jit(solution)/shard_map/queries/pallas_call | solution.py:267
  52.6 0.0 copy-start
  52.6 11.9 %all_to_all.33 = f32[32,5,2,128]{3,2,1,0:T(2,128)S(1)} all-to-all(f32[32,5,2,128]{3,2,1,0:T(2,128)S(1)} %bitcast.22), channel_id=1, replica_groups=mesh['x'=4,'z'=8,'c'=2,'space'=4] {'x','c','space'}, dimensions={0} | all-to-all | bytes 327680 | tf_op jit(solution)/shard_map/all_to_all | solution.py:246
  64.5 11.3 %all_to_all.34 = f32[8,20,2,128]{3,2,1,0:T(2,128)S(1)} all-to-all(f32[8,20,2,128]{3,2,1,0:T(2,128)S(1)} %bitcast.21), channel_id=1, replica_groups=mesh['x'=4,'z'=8,'c'=2,'space'=4] {'z'}, dimensions={0} | all-to-all | bytes 327680 | tf_op jit(solution)/shard_map/all_to_all | solution.py:246
  75.8 12.5 %all_to_all.35 = f32[32,5,2,128]{3,2,1,0:T(2,128)S(1)} all-to-all(f32[32,5,2,128]{3,2,1,0:T(2,128)S(1)} %bitcast.19), channel_id=1, replica_groups=mesh['x'=4,'z'=8,'c'=2,'space'=4] {'x','c','space'}, dimensions={0} | all-to-all | bytes 327680 | tf_op jit(solution)/shard_map/all_to_all | solution.py:246
  88.4 0.0 copy-done.1
  88.4 0.0 copy-done
  88.4 2.3 %keys.1 = (bf16[1,512,1152]{2,1,0:T(8,128)(2,1)}, bf16[1,512,1152]{2,1,0:T(8,128)(2,1)}) custom-call(bf16[1,512,1152]{2,1,0:T(8,128)(2,1)S(1)} %copy-done, bf16[1,512,1152]{2,1,0:T(8,128)(2,1)S(1)} %copy-done.1, f32[320,128]{1,0:T(8,128)S(1)} %bitcast.13), custom_call_target="tpu_custom_call" | custom-call | tf_op jit(solution)/shard_map/keys/pallas_call | solution.py:281
  (4 shorter events, 0.1 us)
Async XLA Ops:
  0.6 48.9 %copy-start.3 = (bf16[1,512,1152]{2,1,0:T(8,128)(2,1)S(1)}, bf16[1,512,1152]{2,1,0:T(8,128)(2,1)}, u32[]{:S(2)}) copy-start(bf16[1,512,1152]{2,1,0:T(8,128)(2,1)} %grad_ref.1) | copy-start | bytes 3538948
  3.4 46.2 %copy-start.2 = (bf16[1,512,1152]{2,1,0:T(8,128)(2,1)S(1)}, bf16[1,512,1152]{2,1,0:T(8,128)(2,1)}, u32[]{:S(2)}) copy-start(bf16[1,512,1152]{2,1,0:T(8,128)(2,1)} %query_ref.1) | copy-start | bytes 3538948
  49.6 38.8 %copy-start.1 = (bf16[1,512,1152]{2,1,0:T(8,128)(2,1)S(1)}, bf16[1,512,1152]{2,1,0:T(8,128)(2,1)}, u32[]{:S(2)}) copy-start(bf16[1,512,1152]{2,1,0:T(8,128)(2,1)} %value_ref.1) | copy-start | bytes 3538948
  52.6 35.8 %copy-start = (bf16[1,512,1152]{2,1,0:T(8,128)(2,1)S(1)}, bf16[1,512,1152]{2,1,0:T(8,128)(2,1)}, u32[]{:S(2)}) copy-start(bf16[1,512,1152]{2,1,0:T(8,128)(2,1)} %key_ref.1) | copy-start | bytes 3538948

commit v6 on v5

--- a/solution.py
+++ b/solution.py
@@ -87,11 +87,14 @@
     for i, rows in enumerate(pieces):
         copies[2 * i].wait()
         copies[2 * i + 1].wait()
+        feats = [jnp.maximum(key_ref[0, rows, lanes_of(group)], 0) for group in range(GROUPS)]
+        fulls = [
+            dot(feats[group], value_ref[0, rows, lanes_of(group)], ROW_BY_ROW)
+            for group in range(GROUPS)
+        ]
         for group in range(GROUPS):
-            feat = jnp.maximum(key_ref[0, rows, lanes_of(group)], 0)
-            full = dot(feat, value_ref[0, rows, lanes_of(group)], ROW_BY_ROW)
-            state = gather_heads(full, same)
-            norm = jnp.sum(feat.astype(jnp.float32), axis=0, keepdims=True)
+            norm = jnp.sum(feats[group].astype(jnp.float32), axis=0, keepdims=True)
+            state = gather_heads(fulls[group], same)
             if i:
                 state = state + out_ref[state_of(group), :]
                 norm = norm + out_ref[norm_of(group), :]

time: 91 us -> 91 us (level)
  no operation moved by 1% of the time
where the time goes in v6:
time: 91 us; the launch traced here: 90.7 us
  blocking collectives  81.8 us (90%)
  Pallas kernels  8.18 us (9%)
    all_to_all x6, blocking collectives, exchange(): return lax.all_to_all(pieces, axes, 0, 0, tiled=True).reshape(ROWS, LANES)  81.8 us
    pallas_call x1, Pallas kernels, shards(): pl.pallas_call(query_kernel, in_specs=[vmem] * 3, out_specs=(hbm, vmem),...  3.01 us
    pallas_call x1, Pallas kernels, shards(): pl.pallas_call(block_kernel, in_specs=[hbm, hbm], out_specs=vmem, out_sha...  2.75 us
    pallas_call x1, Pallas kernels, shards(): pl.pallas_call(key_kernel, in_specs=[vmem] * 3, out_specs=(hbm, hbm), out...  2.27 us

profile of v6, /device:TPU:1, one launch (start us, length us, event | category | flops | bytes accessed | tf_op | source)
XLA Modules:
  0.0 90.7 jit_solution(5326698013801147810)
XLA Ops:
  0.6 0.0 copy-start.3
  0.6 2.8 %blocks.1 = f32[320,128]{1,0:T(8,128)} custom-call(bf16[1,512,1152]{2,1,0:T(8,128)(2,1)} %key_ref.1, bf16[1,512,1152]{2,1,0:T(8,128)(2,1)} %value_ref.1), custom_call_target="tpu_custom_call" | custom-call | tf_op jit(solution)/shard_map/blocks/pallas_call | solution.py:260
  3.4 0.0 copy-start.2
  3.4 16.6 %all_to_all.30 = f32[32,5,2,128]{3,2,1,0:T(2,128)S(1)} all-to-all(f32[32,5,2,128]{3,2,1,0:T(2,128)} %bitcast.23), channel_id=1, replica_groups=mesh['x'=4,'z'=8,'c'=2,'space'=4] {'x','c','space'}, dimensions={0} | all-to-all | bytes 327680 | tf_op jit(solution)/shard_map/all_to_all | solution.py:249
  20.1 16.4 %all_to_all.31 = f32[8,20,2,128]{3,2,1,0:T(2,128)S(1)} all-to-all(f32[8,20,2,128]{3,2,1,0:T(2,128)S(1)} %bitcast.20), channel_id=1, replica_groups=mesh['x'=4,'z'=8,'c'=2,'space'=4] {'z'}, dimensions={0} | all-to-all | bytes 327680 | tf_op jit(solution)/shard_map/all_to_all | solution.py:249
  36.5 13.1 %all_to_all.32 = f32[32,5,2,128]{3,2,1,0:T(2,128)S(1)} all-to-all(f32[32,5,2,128]{3,2,1,0:T(2,128)S(1)} %bitcast.18), channel_id=1, replica_groups=mesh['x'=4,'z'=8,'c'=2,'space'=4] {'x','c','space'}, dimensions={0} | all-to-all | bytes 327680 | tf_op jit(solution)/shard_map/all_to_all | solution.py:249
  49.6 0.0 copy-done.3
  49.6 0.0 copy-done.2
  49.6 0.0 copy-start.1
  49.6 3.0 %queries.1 = (bf16[1,512,1152]{2,1,0:T(8,128)(2,1)}, f32[320,128]{1,0:T(8,128)S(1)}) custom-call(bf16[1,512,1152]{2,1,0:T(8,128)(2,1)S(1)} %copy-done.2, bf16[1,512,1152]{2,1,0:T(8,128)(2,1)S(1)} %copy-done.3, f32[320,128]{1,0:T(8,128)S(1)} %bitcast.12), custom_call_target="tpu_custom_call" | custom-call | tf_op jit(solution)/shard_map/queries/pallas_call | solution.py:270
  52.6 0.0 copy-start
  52.6 11.9 %all_to_all.33 = f32[32,5,2,128]{3,2,1,0:T(2,128)S(1)} all-to-all(f32[32,5,2,128]{3,2,1,0:T(2,128)S(1)} %bitcast.22), channel_id=1, replica_groups=mesh['x'=4,'z'=8,'c'=2,'space'=4] {'x','c','space'}, dimensions={0} | all-to-all | bytes 327680 | tf_op jit(solution)/shard_map/all_to_all | solution.py:249
  64.5 11.3 %all_to_all.34 = f32[8,20,2,128]{3,2,1,0:T(2,128)S(1)} all-to-all(f32[8,20,2,128]{3,2,1,0:T(2,128)S(1)} %bitcast.21), channel_id=1, replica_groups=mesh['x'=4,'z'=8,'c'=2,'space'=4] {'z'}, dimensions={0} | all-to-all | bytes 327680 | tf_op jit(solution)/shard_map/all_to_all | solution.py:249
  75.8 12.5 %all_to_all.35 = f32[32,5,2,128]{3,2,1,0:T(2,128)S(1)} all-to-all(f32[32,5,2,128]{3,2,1,0:T(2,128)S(1)} %bitcast.19), channel_id=1, replica_groups=mesh['x'=4,'z'=8,'c'=2,'space'=4] {'x','c','space'}, dimensions={0} | all-to-all | bytes 327680 | tf_op jit(solution)/shard_map/all_to_all | solution.py:249
  88.4 0.0 copy-done.1
  88.4 0.0 copy-done
  88.4 2.3 %keys.1 = (bf16[1,512,1152]{2,1,0:T(8,128)(2,1)}, bf16[1,512,1152]{2,1,0:T(8,128)(2,1)}) custom-call(bf16[1,512,1152]{2,1,0:T(8,128)(2,1)S(1)} %copy-done, bf16[1,512,1152]{2,1,0:T(8,128)(2,1)S(1)} %copy-done.1, f32[320,128]{1,0:T(8,128)S(1)} %bitcast.13), custom_call_target="tpu_custom_call" | custom-call | tf_op jit(solution)/shard_map/keys/pallas_call | solution.py:284
  (4 shorter events, 0.1 us)
Async XLA Ops:
  0.6 48.9 %copy-start.3 = (bf16[1,512,1152]{2,1,0:T(8,128)(2,1)S(1)}, bf16[1,512,1152]{2,1,0:T(8,128)(2,1)}, u32[]{:S(2)}) copy-start(bf16[1,512,1152]{2,1,0:T(8,128)(2,1)} %grad_ref.1) | copy-start | bytes 3538948
  3.4 46.2 %copy-start.2 = (bf16[1,512,1152]{2,1,0:T(8,128)(2,1)S(1)}, bf16[1,512,1152]{2,1,0:T(8,128)(2,1)}, u32[]{:S(2)}) copy-start(bf16[1,512,1152]{2,1,0:T(8,128)(2,1)} %query_ref.1) | copy-start | bytes 3538948
  49.6 38.8 %copy-start.1 = (bf16[1,512,1152]{2,1,0:T(8,128)(2,1)S(1)}, bf16[1,512,1152]{2,1,0:T(8,128)(2,1)}, u32[]{:S(2)}) copy-start(bf16[1,512,1152]{2,1,0:T(8,128)(2,1)} %value_ref.1) | copy-start | bytes 3538948
  52.6 35.8 %copy-start = (bf16[1,512,1152]{2,1,0:T(8,128)(2,1)S(1)}, bf16[1,512,1152]{2,1,0:T(8,128)(2,1)}, u32[]{:S(2)}) copy-start(bf16[1,512,1152]{2,1,0:T(8,128)(2,1)} %key_ref.1) | copy-start | bytes 3538948
